TPU v7x, 32 devices: a whole 2x2x4 slice. The times are simulated.
32 devices in a mesh: dp: 4 (over x, core), expert: 8 (over z, y).
Axes of the slice: x: 2, y: 2, z: 4, core: 2. Of those that a mesh axis runs over, the one named last changes fastest.
Arguments:
- tokens: bfloat16 [4096, 4096], P(('dp', 'expert')), may hold values from -6 to 6
- output_gradient: bfloat16 [4096, 4096], P(('dp', 'expert')), may hold values from -6 to 6
- slot: int32 [4096, 1], P(('dp', 'expert')), may hold values from -1 to 7, as said below
- gate_weight: float32 [4096, 1], P(('dp', 'expert')), may hold values from 0.2 to 1
- gate_up_weight: bfloat16 [8, 4096, 384], P('expert', 'dp'), may hold values from -0.09375 to 0.09375
- down_weight: bfloat16 [8, 192, 4096], P('expert', None, 'dp'), may hold values from -0.15625 to 0.15625
Outputs:
- grad_tokens: bfloat16 [4096, 4096], P(('dp', 'expert'))
- grad_gate_up: bfloat16 [8, 4096, 384], P('expert', 'dp')
Inputs may be any that keep to these rules, and one draw needn't show every extreme that they name: `slot`: within the tokens of one block of 128 and one window expert, the values other than -1 are 0, 1, ..., k - 1, each once; one window expert, the same one in every block, takes all 8 slots in every block, and each of the other window experts takes at most 4 slots in that block.
All inputs are finite; a program needn't handle non-finite values.
Results may differ from a plain program's by a relative error of at most 0.022.
Values may be sent and summed in bfloat16 or wider, within the bound.
A program may use at most 64 MiB of HBM per device.

v0:
```python
import jax
import jax.numpy as jnp
from jax import lax
from jax.sharding import PartitionSpec as P

GROUP = 8
CAP = 8


def sum_gate_up(x_mat, dgu):
    part_gu = lax.dot_general(
        x_mat, dgu, (((0,), (0,)), ((), ())), preferred_element_type=jnp.float32
    )
    return lax.psum_scatter(
        part_gu.astype(jnp.bfloat16), "dp", scatter_dimension=0, tiled=True
    ).astype(jnp.float32)


def on_device(tokens, output_gradient, slot, gate_weight, gate_up_weight, down_weight):
    expert_windows = slot.shape[1]
    width = tokens.shape[1]
    positions = jnp.arange(CAP, dtype=jnp.int32)
    selector = jnp.transpose(slot)[:, None, :] == positions[None, :, None]
    picked_experts = selector.astype(jnp.bfloat16)
    sent_x = jnp.einsum(
        "ect,td->ecd", picked_experts, tokens, preferred_element_type=jnp.float32
    ).astype(jnp.bfloat16)
    picked_dy = jnp.einsum(
        "ect,td->ecd", picked_experts, output_gradient, preferred_element_type=jnp.float32
    )
    selected_gate = jnp.sum(
        jnp.where(selector, jnp.transpose(gate_weight)[:, None, :], 0.0), axis=2
    )
    sent_g = (picked_dy * selected_gate[..., None]).astype(jnp.bfloat16)
    copies_x = jnp.repeat(sent_x, GROUP, axis=0)
    copies_g = jnp.repeat(sent_g, GROUP, axis=0)
    recv_x, received_gradient = (
        lax.all_to_all(copies_x, "expert", split_axis=0, concat_axis=0, tiled=True),
        lax.all_to_all(copies_g, "expert", split_axis=0, concat_axis=0, tiled=True),
    )
    full_gu = lax.all_gather(gate_up_weight[0], "dp", axis=0, tiled=True)
    full_down = lax.all_gather(down_weight[0], "dp", axis=1, tiled=True)
    x_mat = recv_x.reshape(-1, width)
    joined = jnp.dot(x_mat, full_gu, preferred_element_type=jnp.float32)
    half = full_gu.shape[1] // 2
    pre = joined[:, :half]
    up_part = joined[:, half:]
    sig = jax.nn.sigmoid(pre)
    act = pre * sig
    g_mat = received_gradient.reshape(-1, width)
    dh_rows = lax.dot_general(
        g_mat, full_down, (((1,), (1,)), ((), ())), preferred_element_type=jnp.float32
    )
    dgate = dh_rows * up_part * sig * (1.0 + pre * (1.0 - sig))
    dup = dh_rows * act
    dgu = jnp.concatenate([dgate, dup], axis=1).astype(jnp.bfloat16)
    dx_part = lax.dot_general(
        dgu, full_gu, (((1,), (1,)), ((), ())), preferred_element_type=jnp.float32
    ).astype(jnp.bfloat16)
    back = lax.all_to_all(
        dx_part.reshape(recv_x.shape), "expert", split_axis=0, concat_axis=0, tiled=True
    )
    gu_sum = sum_gate_up(x_mat, dgu)
    summed = jnp.sum(back.astype(jnp.float32).reshape(expert_windows, GROUP, CAP, width), axis=1)
    grad_tokens = jnp.einsum("ect,ecd->td", selector.astype(jnp.float32), summed).astype(
        jnp.bfloat16
    )
    return (grad_tokens, gu_sum.astype(jnp.bfloat16)[None])


def solution(mesh):
    in_specs = (
        P(("dp", "expert"), None),
        P(("dp", "expert"), None),
        P(("dp", "expert"), None),
        P(("dp", "expert"), None),
        P("expert", "dp", None),
        P("expert", None, "dp"),
    )
    out_specs = (P(("dp", "expert"), None), P("expert", "dp", None))
    return jax.shard_map(
        on_device, mesh=mesh, in_specs=in_specs, out_specs=out_specs, check_vma=False
    )
```

profile of v0, /device:TPU:0, one launch (start us, length us, event | category | flops | bytes accessed | tf_op | source)
XLA Modules:
  0.0 111.5 jit_solution(16282392650941002108)
XLA Ops:
  7.2 0.0 copy-start
  7.2 0.0 copy-start.2
  7.2 0.0 copy-start.3
  7.2 0.0 copy-start.1
  7.2 0.0 all-gather.7.cloned.1.call-start
  7.3 0.7 all-gather.7.cloned.1.call-update
  7.9 0.0 all-gather.5.cloned.1.call-start
  8.0 0.7 all-gather.5.cloned.1.call-update
  8.7 0.0 copy-done
  8.7 0.9 convolution_convert_fusion.3
  9.6 0.8 reshape.142
  10.4 7.3 %all-to-all-start.1 = ((bf16[8,8,4096]{2,1,0:T(8,128)(2,1)}), bf16[8,8,4096]{2,1,0:T(8,128)(2,1)S(1)}, u32[]{:S(2)}, u32[]{:S(2)}) async-start(bf16[8,8,4096]{2,1,0:T(8,128)(2,1)} %reshape.142), calls=%async_computation.1 | async-start | bytes 1048576 | tf_op jit(solution)/shard_map/all_to_all | solution.py:38
  17.7 0.0 copy-done.2
  17.7 0.0 copy-done.3
  17.7 0.1 select_reduce_fusion
  17.9 0.3 fusion.1
  18.1 14.1 %all-to-all-done.1 = bf16[8,8,4096]{2,1,0:T(8,128)(2,1)S(1)} async-done(((bf16[8,8,4096]{2,1,0:T(8,128)(2,1)}), bf16[8,8,4096]{2,1,0:T(8,128)(2,1)S(1)}, u32[]{:S(2)}, u32[]{:S(2)}) %all-to-all-start.1) | async-done | bytes 524320 | tf_op jit(solution)/shard_map/all_to_all | solution.py:38
  32.2 0.8 reshape.140
  33.0 3.6 %all-to-all-start = ((bf16[8,8,4096]{2,1,0:T(8,128)(2,1)}), bf16[8,8,4096]{2,1,0:T(8,128)(2,1)S(1)}, u32[]{:S(2)}, u32[]{:S(2)}) async-start(bf16[8,8,4096]{2,1,0:T(8,128)(2,1)} %reshape.140), calls=%async_computation | async-start | bytes 1048576 | tf_op jit(solution)/shard_map/all_to_all | solution.py:39
  36.7 0.0 reduce-scatter.2.cloned.1.call-start
  36.7 4.1 %all-gather.7.cloned.1.call-done = bf16[1,4096,384]{2,1,0:T(8,128)(2,1)} async-done(((bf16[1,1024,384]{2,1,0:T(8,128)(2,1)}), bf16[1,4096,384]{2,1,0:T(8,128)(2,1)}) %all-gather.7.cloned.1.call-update) | async-done | bytes 3145744 | tf_op jit(solution)/shard_map/all_gather | solution.py:41
  40.9 2.5 %fusion.3 = f32[64,384]{1,0:T(8,128)S(1)} fusion(bf16[1,4096,384]{2,1,0:T(8,128)(2,1)} %all-gather.7.cloned.1.call-done, bf16[8,8,4096]{2,1,0:T(8,128)(2,1)S(1)} %all-to-all-done.1), kind=kOutput, calls=%fused_computation.8 | convolution fusion | flops 201326592 | bytes 3768320 | tf_op jit(solution)/shard_map/dot_general | solution.py:44
  43.3 8.0 %all-to-all-done = bf16[8,8,4096]{2,1,0:T(8,128)(2,1)S(1)} async-done(((bf16[8,8,4096]{2,1,0:T(8,128)(2,1)}), bf16[8,8,4096]{2,1,0:T(8,128)(2,1)S(1)}, u32[]{:S(2)}, u32[]{:S(2)}) %all-to-all-start) | async-done | bytes 524320 | tf_op jit(solution)/shard_map/all_to_all | solution.py:39
  51.3 10.8 %all-gather.5.cloned.1.call-done = bf16[1,192,4096]{2,1,0:T(8,128)(2,1)} async-done(((bf16[1,192,1024]{2,1,0:T(8,128)(2,1)}), bf16[1,192,4096]{2,1,0:T(8,128)(2,1)}) %all-gather.5.cloned.1.call-update) | async-done | bytes 1572880 | tf_op jit(solution)/shard_map/all_gather | solution.py:42
  62.1 2.0 %fusion.12 = (bf16[64,192]{1,0:T(8,128)(2,1)S(1)}, bf16[64,192]{1,0:T(8,128)(2,1)S(1)}) fusion(f32[64,384]{1,0:T(8,128)S(1)} %fusion.3, bf16[1,192,4096]{2,1,0:T(8,128)(2,1)} %all-gather.5.cloned.1.call-done, bf16[8,8,4096]{2,1,0:T(8,128)(2,1)S(1)} %all-to-all-done), kind=kOutput, calls=%fused_computation.19 | convolution fusion | flops 100823040 | bytes 2244608 | tf_op jit(solution)/shard_map/dot_general | solution.py:51
  64.2 2.7 %convolution_convert_fusion = bf16[4096,384]{1,0:T(8,128)(2,1)} fusion(bf16[8,8,4096]{2,1,0:T(8,128)(2,1)S(1)} %all-to-all-done.1, bf16[64,192]{1,0:T(8,128)(2,1)S(1)} %get-tuple-element.3, bf16[64,192]{1,0:T(8,128)(2,1)S(1)} %get-tuple-element.2), kind=kOutput, calls=%fused_computation | convolution fusion | flops 202997760 | bytes 3719168 | tf_op jit(solution)/shard_map/dot_general | solution.py:11
  66.9 0.0 reduce-scatter.2.cloned.1.call-update
  66.9 3.0 %fusion = bf16[8,8,4096]{2,1,0:T(8,128)(2,1)S(1)} fusion(bf16[1,4096,384]{2,1,0:T(8,128)(2,1)} %all-gather.7.cloned.1.call-done, bf16[64,192]{1,0:T(8,128)(2,1)S(1)} %get-tuple-element.3, bf16[64,192]{1,0:T(8,128)(2,1)S(1)} %get-tuple-element.2), kind=kOutput, calls=%fused_computation.3 | convolution fusion | flops 201687040 | bytes 3719168 | tf_op jit(solution)/shard_map/dot_general | solution.py:57
  69.9 20.2 %all_to_all.15 = bf16[8,8,4096]{2,1,0:T(8,128)(2,1)S(1)} all-to-all(bf16[8,8,4096]{2,1,0:T(8,128)(2,1)S(1)} %fusion), channel_id=1, replica_groups=mesh['dp'=4,'expert'=8] {'expert'}, dimensions={0} | all-to-all | bytes 1048576 | tf_op jit(solution)/shard_map/all_to_all | solution.py:60
  90.1 0.1 convert_reduce_fusion
  90.2 1.5 %convolution_convert_fusion.1 = bf16[128,4096]{1,0:T(8,128)(2,1)} fusion(bf16[8,4096]{1,0:T(8,128)(2,1)S(1)} %convert_reduce_fusion, s32[128]{0:T(128)S(1)} %bitcast.31), kind=kOutput, calls=%fused_computation.1 | convolution fusion | flops 8389632 | bytes 1114624 | tf_op jit(solution)/shard_map/ect,ecd->td/dot_general | solution.py:65
  91.7 13.3 %reduce-scatter.2.cloned.1.call-done = bf16[1024,384]{1,0:T(8,128)(2,1)} async-done(((bf16[4096,384]{1,0:T(8,128)(2,1)}), bf16[1024,384]{1,0:T(8,128)(2,1)}) %reduce-scatter.2.cloned.1.call-update) | async-done | bytes 786448 | tf_op jit(solution)/shard_map/reduce_scatter | solution.py:14
  (1 shorter events, 0.0 us)
Async XLA Ops:
  7.2 1.5 %copy-start = (bf16[128,4096]{1,0:T(8,128)(2,1)S(1)}, bf16[128,4096]{1,0:T(8,128)(2,1)}, u32[]{:S(2)}) copy-start(bf16[128,4096]{1,0:T(8,128)(2,1)} %param.6) | copy-start | bytes 3145732
  7.2 10.5 %copy-start.2 = (s32[128,1]{0,1:T(1,128)S(1)}, s32[128,1]{0,1:T(1,128)}, u32[]{:S(2)}) copy-start(s32[128,1]{0,1:T(1,128)} %param.8) | copy-start | bytes 1540
  7.2 10.5 %copy-start.3 = (f32[128,1]{0,1:T(1,128)S(1)}, f32[128,1]{0,1:T(1,128)}, u32[]{:S(2)}) copy-start(f32[128,1]{0,1:T(1,128)} %param.9) | copy-start | bytes 1540
  7.2 10.7 %copy-start.1 = (bf16[128,4096]{1,0:T(8,128)(2,1)S(1)}, bf16[128,4096]{1,0:T(8,128)(2,1)}, u32[]{:S(2)}) copy-start(bf16[128,4096]{1,0:T(8,128)(2,1)} %param.7) | copy-start | bytes 3145732
  7.2 33.7 %all-gather.7.cloned.1.call-start = ((), (), s32[]{:S(2)}) async-start(), calls=%async_computation.6 | async-start | bytes 3932160 | tf_op jit(solution)/shard_map/all_gather | solution.py:41
  7.9 54.2 %all-gather.5.cloned.1.call-start = ((), (), s32[]{:S(2)}) async-start(), calls=%async_computation.5 | async-start | bytes 1966080 | tf_op jit(solution)/shard_map/all_gather | solution.py:42
  10.4 21.8 %all-to-all-start.1 = ((bf16[8,8,4096]{2,1,0:T(8,128)(2,1)}), bf16[8,8,4096]{2,1,0:T(8,128)(2,1)S(1)}, u32[]{:S(2)}, u32[]{:S(2)}) async-start(bf16[8,8,4096]{2,1,0:T(8,128)(2,1)} %reshape.142), calls=%async_computation.1 | async-start | bytes 1048576 | tf_op jit(solution)/shard_map/all_to_all | solution.py:38
  33.0 18.3 %all-to-all-start = ((bf16[8,8,4096]{2,1,0:T(8,128)(2,1)}), bf16[8,8,4096]{2,1,0:T(8,128)(2,1)S(1)}, u32[]{:S(2)}, u32[]{:S(2)}) async-start(bf16[8,8,4096]{2,1,0:T(8,128)(2,1)} %reshape.140), calls=%async_computation | async-start | bytes 1048576 | tf_op jit(solution)/shard_map/all_to_all | solution.py:39
  36.7 68.3 %reduce-scatter.2.cloned.1.call-start = ((), (), s32[]{:S(2)}) async-start(), calls=%async_computation.4 | async-start | bytes 3932160 | tf_op jit(solution)/shard_map/reduce_scatter | solution.py:14
Sparse Core Ops, SparseCore 0:
  9.6 31.2 all-gather.6
  42.4 19.6 all-gather.4
  67.0 37.9 reduce-scatter.1
where the time goes:
time: 112 us
  waiting for transfers between devices  51.8 us (46%)
  blocking collectives  20.2 us (18%)
  between operations  13.8 us (12%)
  matrix products  12.9 us (12%)
  starting transfers between devices  11 us (10%)
  local copies, waits for them, and re-layouts  1.69 us (2%)
    all_to_all x1, blocking collectives, on_device(): lax.all_to_all(dx_part.reshape(recv_x.shape), 'expert', split_axis=0, con...  20.2 us
    all_to_all x1, waiting for transfers between devices, on_device(): lax.all_to_all(copies_x, 'expert', split_axis=0, concat_axis=0, tiled=True)  14.1 us
    reduce_scatter x1, waiting for transfers between devices, sum_gate_up(): lax.psum_scatter(part_gu.astype(jnp.bfloat16), 'dp', scatter_dimension=0,...  13.3 us
    all_gather x1, waiting for transfers between devices, on_device(): full_down = lax.all_gather(down_weight[0], 'dp', axis=1, tiled=True)  10.8 us
    all_to_all x1, waiting for transfers between devices, on_device(): lax.all_to_all(copies_g, 'expert', split_axis=0, concat_axis=0, tiled=True)  8.01 us
    all_to_all x1, starting transfers between devices, on_device(): lax.all_to_all(copies_x, 'expert', split_axis=0, concat_axis=0, tiled=True)  7.28 us
    all_gather x1, waiting for transfers between devices, on_device(): full_gu = lax.all_gather(gate_up_weight[0], 'dp', axis=0, tiled=True)  4.15 us
    all_to_all x1, starting transfers between devices, on_device(): lax.all_to_all(copies_g, 'expert', split_axis=0, concat_axis=0, tiled=True)  3.64 us
  transfers between devices with their start and end apart: 5, of which 5 were waited for; matrix products, arithmetic and copies ran while one was open for 9% of the time, Pallas kernels for 0%

commit v1 on v0

v1 whole, which is shorter than its diff:
```python
import functools

import jax
import jax.numpy as jnp
from jax import lax
from jax.experimental import pallas as pl
from jax.experimental.pallas import tpu as pltpu
from jax.sharding import PartitionSpec as P

GROUP = 8
CAP = 8
MESH = pl.DeviceIdType.MESH
F32 = jnp.float32
BF16 = jnp.bfloat16
NT = (((1,), (1,)), ((), ()))
TN = (((0,), (0,)), ((), ()))


def kernel(
    n_dp, windows,
    tok_ref, dy_ref, slot_ref, gate_ref, gu_ref, down_ref,
    gx_ref, gw_ref,
    pick, buf, xall, part, prcv, dgrcv, dguall, dxs, ret, back, fin,
    s_pick, r_pick, s_ag, r_ag, s_rs, r_rs, s_dg, r_dg, s_ret, r_ret, s_fin, r_fin,
):
    S = GROUP
    Z = S // 2
    W = windows
    n_same = n_dp * W
    tokens, width = tok_ref.shape
    cols = width // n_dp
    hidden = down_ref.shape[0]
    rows = n_dp * W * CAP
    me_d = lax.axis_index("dp")
    me_x = lax.axis_index("expert")
    me_w = me_x // S
    me_s = me_x % S
    zz = me_s // 2
    yy = me_s % 2

    def member(s):
        return (me_d, me_w * S + s)

    barrier = pltpu.get_barrier_semaphore()

    def same(k):
        flat = (me_d * W + me_w + k) % n_same
        return flat // W, flat % W

    for k in range(1, n_same):
        d, w = same(k)
        pl.semaphore_signal(barrier, inc=1, device_id=(d, w * S + me_s), device_id_type=MESH)
    for k in range(1, S):
        pl.semaphore_signal(barrier, inc=1, device_id=member((me_s + k) % S), device_id_type=MESH)

    lane = lax.broadcasted_iota(jnp.int32, (tokens, 128), 1)
    for e in range(W):
        hit = slot_ref[:, e : e + 1] == lane
        sel = jnp.where(hit, 1.0, 0.0).T[:CAP]
        weight = jnp.sum(jnp.where(hit, gate_ref[:, e : e + 1], 0.0).T[:CAP], axis=1, keepdims=True)
        sel = sel.astype(BF16)
        for d in range(n_dp):
            cut = slice(d * cols, (d + 1) * cols)
            x = jnp.dot(sel, tok_ref[:, cut], preferred_element_type=F32)
            g = jnp.dot(sel, dy_ref[:, cut], preferred_element_type=F32) * weight
            pick[d, e] = jnp.concatenate([x, g], axis=0).astype(BF16)
    pl.semaphore_wait(barrier, n_same - 1 + S - 1)

    def pick_copy(d, w):
        return pltpu.make_async_remote_copy(
            src_ref=pick.at[d, w], dst_ref=buf.at[me_s, me_d, me_w],
            send_sem=s_pick.at[d, w], recv_sem=r_pick.at[me_d, me_w],
            device_id=(d, w * S + me_s), device_id_type=MESH,
        )

    def pick_arrival(d, w):
        return pltpu.make_async_remote_copy(
            src_ref=pick.at[d, w], dst_ref=buf.at[me_s, d, w],
            send_sem=s_pick.at[d, w], recv_sem=r_pick.at[d, w],
            device_id=(d, w * S + me_s), device_id_type=MESH,
        )

    for k in range(1, n_same):
        pick_copy(*same(k)).start()
    buf[me_s, me_d, me_w] = pick[me_d, me_w]
    for k in range(1, n_same):
        pick_arrival(*same(k)).wait_recv()

    def spread(slot, way, target):
        return pltpu.make_async_remote_copy(
            src_ref=buf.at[slot], dst_ref=buf.at[slot],
            send_sem=s_ag.at[slot, way], recv_sem=r_ag.at[slot],
            device_id=member(target), device_id_type=MESH,
        )

    def reduce_copy(slot, d, owner):
        return pltpu.make_async_remote_copy(
            src_ref=part.at[slot, d], dst_ref=prcv.at[slot, owner],
            send_sem=s_rs.at[slot, d], recv_sem=r_rs.at[slot, owner],
            device_id=(d, me_x), device_id_type=MESH,
        )

    def share_copy(slot, d, owner):
        return pltpu.make_async_remote_copy(
            src_ref=dgrcv.at[slot, me_d], dst_ref=dgrcv.at[slot, owner],
            send_sem=s_dg.at[slot, d], recv_sem=r_dg.at[slot, owner],
            device_id=(d, me_x), device_id_type=MESH,
        )

    def return_copy(slot, owner):
        return pltpu.make_async_remote_copy(
            src_ref=dxs.at[slot], dst_ref=ret.at[owner],
            send_sem=s_ret.at[slot], recv_sem=r_ret.at[owner],
            device_id=member(slot), device_id_type=MESH,
        )

    near = jnp.minimum(zz, Z - 1 - zz)

    def nth(n):
        m = n // 2
        alternating = ((m + 1) // 2) * (1 - 2 * (m % 2))
        far = m - near
        beyond = jnp.where(zz > Z - 1 - zz, -far, far)
        delta = jnp.where(m <= 2 * near, alternating, beyond)
        own = n % 2 == 0
        return delta, own, (zz + delta) * 2 + jnp.where(own, yy, 1 - yy)

    def up(delta, own):
        return own & (delta <= 0) & (zz + 1 < Z)

    def down(delta, own):
        return own & (delta >= 0) & (zz >= 1)

    def arrive(n):
        delta, own, slot = nth(n)

        @pl.when(n > 0)
        def _():
            spread(slot, 0, (me_s + 1) % S).wait_recv()

        @pl.when(up(delta, own))
        def _():
            spread(slot, 0, me_s + 2).start()

        @pl.when(down(delta, own))
        def _():
            spread(slot, 1, me_s - 2).start()

        @pl.when(own)
        def _():
            spread(slot, 2, zz * 2 + 1 - yy).start()

        both = buf[slot].astype(F32).reshape(n_dp * W, 2, CAP, cols)
        x = both[:, 0].reshape(rows, cols).astype(BF16)
        g = both[:, 1].reshape(rows, cols).astype(BF16)
        xall[slot] = x
        a_u = jnp.dot(x, gu_ref[...], preferred_element_type=F32)
        dh = lax.dot_general(g, down_ref[...], NT, preferred_element_type=F32)
        part[slot, :, :, : 2 * hidden] = a_u.reshape(n_dp, W * CAP, 2 * hidden)
        part[slot, :, :, 2 * hidden :] = dh.reshape(n_dp, W * CAP, hidden)
        for k in range(1, n_dp):
            reduce_copy(slot, (me_d + k) % n_dp, me_d).start()

    def activate(n):
        _, _, slot = nth(n)
        total = part[slot, me_d]
        for k in range(1, n_dp):
            d = (me_d + k) % n_dp
            reduce_copy(slot, d, d).wait_recv()
            total = total + prcv[slot, d]
        pre = total[:, :hidden]
        up_part = total[:, hidden : 2 * hidden]
        dh = total[:, 2 * hidden :]
        sig = jax.nn.sigmoid(pre)
        dgate = dh * up_part * sig * (1.0 + pre * (1.0 - sig))
        dup = dh * (pre * sig)
        dgrcv[slot, me_d] = jnp.concatenate(
            [dgate.reshape(W, CAP, hidden), dup.reshape(W, CAP, hidden)], axis=1
        ).astype(BF16)
        for k in range(1, n_dp):
            share_copy(slot, (me_d + k) % n_dp, me_d).start()

    def give_back(n):
        _, _, slot = nth(n)
        for k in range(1, n_dp):
            d = (me_d + k) % n_dp
            share_copy(slot, d, d).wait_recv()
        both = dgrcv[slot].astype(F32).reshape(n_dp * W, 2, CAP, hidden)
        dgu = jnp.concatenate(
            [both[:, 0].reshape(rows, hidden), both[:, 1].reshape(rows, hidden)], axis=1
        ).astype(BF16)
        dguall[slot] = dgu
        dxs[slot] = lax.dot_general(dgu, gu_ref[...], NT, preferred_element_type=F32).astype(BF16)

        @pl.when(n > 0)
        def _():
            return_copy(slot, me_s).start()

    def step(n, carry):
        @pl.when(n < S)
        def _():
            arrive(n)

        @pl.when((n >= 1) & (n < S + 1))
        def _():
            activate(n - 1)

        @pl.when(n >= 2)
        def _():
            give_back(n - 2)

        return carry

    lax.fori_loop(0, S + 2, step, 0)

    gw_ref[0] = lax.dot_general(
        xall[...].reshape(S * rows, cols), dguall[...].reshape(S * rows, 2 * hidden), TN,
        preferred_element_type=F32,
    ).astype(BF16)

    total = dxs[me_s].astype(F32)
    for k in range(1, S):
        s = (me_s + k) % S
        return_copy(s, s).wait_recv()
        total = total + ret[s].astype(F32)
    total = total.reshape(n_dp, W, CAP, cols)
    back[...] = jnp.concatenate(
        [total[..., : cols // 2], total[..., cols // 2 :]], axis=2
    ).astype(BF16)

    def fin_copy(d, w, owner_d, owner_w):
        return pltpu.make_async_remote_copy(
            src_ref=back.at[d, w], dst_ref=fin.at[owner_d, owner_w],
            send_sem=s_fin.at[d, w], recv_sem=r_fin.at[owner_d, owner_w],
            device_id=(d, w * S + me_s), device_id_type=MESH,
        )

    for k in range(1, n_same):
        d, w = same(k)
        fin_copy(d, w, me_d, me_w).start()
    fin[me_d, me_w] = back[me_d, me_w]
    for k in range(1, n_same):
        d, w = same(k)
        fin_copy(d, w, d, w).wait_recv()

    lane16 = lax.broadcasted_iota(jnp.int32, (tokens, 2 * CAP), 1)
    for d in range(n_dp):
        for h in range(2):
            out = jnp.zeros((tokens, cols // 2), F32)
            for e in range(W):
                hit = slot_ref[:, e : e + 1] == lane16 - h * CAP
                pos = jnp.where(hit & (lane16 >= h * CAP), 1.0, 0.0).astype(BF16)
                out = out + jnp.dot(pos, fin[d, e], preferred_element_type=F32)
            at = d * cols + h * (cols // 2)
            gx_ref[:, at : at + cols // 2] = out.astype(BF16)

    for k in range(1, n_same):
        d, w = same(k)
        pick_copy(d, w).wait_send()
        fin_copy(d, w, me_d, me_w).wait_send()
    for k in range(1, S):
        return_copy((me_s + k) % S, me_s).wait_send()

    def drain(n, carry):
        delta, own, slot = nth(n)

        @pl.when(up(delta, own))
        def _():
            spread(slot, 0, me_s + 2).wait_send()

        @pl.when(down(delta, own))
        def _():
            spread(slot, 1, me_s - 2).wait_send()

        @pl.when(own)
        def _():
            spread(slot, 2, zz * 2 + 1 - yy).wait_send()

        for k in range(1, n_dp):
            d = (me_d + k) % n_dp
            reduce_copy(slot, d, me_d).wait_send()
            share_copy(slot, d, me_d).wait_send()
        return carry

    lax.fori_loop(0, S, drain, 0)


def on_device(n_dp, tokens, output_gradient, slot, gate_weight, gate_up_weight, down_weight):
    W = slot.shape[1]
    S = GROUP
    width = tokens.shape[1]
    _, cols, wide = gate_up_weight.shape
    hidden = wide // 2
    rows = n_dp * W * CAP
    vmem = pl.BlockSpec(memory_space=pltpu.VMEM)
    dma = pltpu.SemaphoreType.DMA
    flops = 2 * S * rows * cols * hidden * 7
    return pl.pallas_call(
        functools.partial(kernel, n_dp, W),
        out_shape=(
            jax.ShapeDtypeStruct(tokens.shape, BF16),
            jax.ShapeDtypeStruct(gate_up_weight.shape, BF16),
        ),
        in_specs=[vmem] * 6,
        out_specs=(vmem, vmem),
        scratch_shapes=[
            pltpu.VMEM((n_dp, W, 2 * CAP, cols), BF16),
            pltpu.VMEM((S, n_dp, W, 2 * CAP, cols), BF16),
            pltpu.VMEM((S, rows, cols), BF16),
            pltpu.VMEM((S, n_dp, W * CAP, 3 * hidden), F32),
            pltpu.VMEM((S, n_dp, W * CAP, 3 * hidden), F32),
            pltpu.VMEM((S, n_dp, W, 2 * CAP, hidden), BF16),
            pltpu.VMEM((S, rows, wide), BF16),
            pltpu.VMEM((S, rows, cols), BF16),
            pltpu.VMEM((S, rows, cols), BF16),
            pltpu.VMEM((n_dp, W, 2 * CAP, cols // 2), BF16),
            pltpu.VMEM((n_dp, W, 2 * CAP, cols // 2), BF16),
            dma((n_dp, W)), dma((n_dp, W)),
            dma((S, 3)), dma((S,)),
            dma((S, n_dp)), dma((S, n_dp)),
            dma((S, n_dp)), dma((S, n_dp)),
            dma((S,)), dma((S,)),
            dma((n_dp, W)), dma((n_dp, W)),
        ],
        compiler_params=pltpu.CompilerParams(
            collective_id=0, has_side_effects=True, vmem_limit_bytes=58 * 1024 * 1024
        ),
        cost_estimate=pl.CostEstimate(
            flops=flops, bytes_accessed=6 * tokens.size + 4 * gate_up_weight.size, transcendentals=0
        ),
        name="routed_backward",
    )(tokens, output_gradient, slot, gate_weight, gate_up_weight[0], down_weight[0])


def solution(mesh):
    in_specs = (
        P(("dp", "expert"), None),
        P(("dp", "expert"), None),
        P(("dp", "expert"), None),
        P(("dp", "expert"), None),
        P("expert", "dp", None),
        P("expert", None, "dp"),
    )
    out_specs = (P(("dp", "expert"), None), P("expert", "dp", None))
    return jax.shard_map(
        functools.partial(on_device, mesh.shape["dp"]),
        mesh=mesh, in_specs=in_specs, out_specs=out_specs, check_vma=False,
    )
```

time: 112 us -> 60.7 us (0.54)
  Pallas kernels: 0 us -> 54.5 us
  waiting for transfers between devices: 51.8 us -> 0 us
  blocking collectives: 20.2 us -> 0 us
  between operations: 13.8 us -> 0.66 us
  matrix products: 12.9 us -> 0 us
  starting transfers between devices: 11 us -> 0 us
  local copies, waits for them, and re-layouts: 1.69 us -> 5.38 us
    pallas_call x0 -> x1, Pallas kernels: none -> 54.5 us  [on_device(): pl.pallas_call(functools.partial(kernel, n_dp, W), out_shape=(jax.ShapeDt...]
    all_to_all x2 -> x0, waiting for transfers between devices: 22.1 us -> none  [the longest x1 14.1 us: on_device(): lax.all_to_all(copies_x, 'expert', split_axis=0, concat_axis=0, tiled=True)]
    all_to_all x1 -> x0, blocking collectives: 20.2 us -> none  [on_device(): lax.all_to_all(dx_part.reshape(recv_x.shape), 'expert', split_axis=0, con...]
    all_gather x2 -> x0, waiting for transfers between devices: 14.9 us -> none  [the longest x1 10.8 us: on_device(): full_down = lax.all_gather(down_weight[0], 'dp', axis=1, tiled=True)]
    reduce_scatter x1 -> x0, waiting for transfers between devices: 13.3 us -> none  [sum_gate_up(): lax.psum_scatter(part_gu.astype(jnp.bfloat16), 'dp', scatter_dimension=0,...]
    dot_general x7 -> x0, matrix products: 12.9 us -> none  [the longest x1 3.01 us: on_device(): lax.dot_general(dgu, full_gu, (((1,), (1,)), ((), ())), preferred_element...]
    all_to_all x2 -> x0, starting transfers between devices: 10.9 us -> none  [the longest x1 7.28 us: on_device(): lax.all_to_all(copies_x, 'expert', split_axis=0, concat_axis=0, tiled=True)]
    unnamed x8 -> x10, local copies, waits for them, and re-layouts: 0.02 us -> 5.38 us
  transfers between devices with their start and end apart: 5 -> 0, of which waited for: 5 -> 0; matrix products, arithmetic and copies ran while one was open for 9% -> 0% of each run, Pallas kernels for 0% -> 0%
where the time goes in v1:
time: 60.7 us; the launch traced here: 60.6 us
  Pallas kernels  54.5 us (90%)
  local copies, waits for them, and re-layouts  5.38 us (9%)
  between operations  0.66 us (1%)
    pallas_call x1, Pallas kernels, on_device(): pl.pallas_call(functools.partial(kernel, n_dp, W), out_shape=(jax.ShapeDt...  54.5 us
    unnamed x10, local copies, waits for them, and re-layouts  5.38 us

profile of v1, /device:TPU:0, one launch (start us, length us, event | category | flops | bytes accessed | tf_op | source)
XLA Modules:
  0.0 60.6 jit_solution(2359507548527651333)
XLA Ops:
  0.6 0.0 copy-start.1
  0.6 0.6 %copy-done.1 = s32[128,1]{0,1:T(1,128)S(1)} copy-done((s32[128,1]{0,1:T(1,128)S(1)}, s32[128,1]{0,1:T(1,128)}, u32[]{:S(2)}) %copy-start.1) | copy-done | bytes 536
  1.3 0.0 copy-start.2
  1.3 0.7 %copy.8.slot_ref = s32[128,1]{1,0:T(8,128)} copy(s32[128,1]{0,1:T(1,128)S(1)} %copy-done.1) | data formatting | bytes 1024 | tf_op args[2]
  2.0 0.0 copy-done.2
  2.0 0.7 %copy.9.gate_ref = f32[128,1]{1,0:T(8,128)} copy(f32[128,1]{0,1:T(1,128)S(1)} %copy-done.2) | data formatting | bytes 1024 | tf_op args[3]
  2.8 54.5 %routed_backward.1 = (bf16[128,4096]{1,0:T(8,128)(2,1)}, bf16[1,1024,384]{2,1,0:T(8,128)(2,1)}) custom-call(bf16[128,4096]{1,0:T(8,128)(2,1)} %tok_ref.1, bf16[128,4096]{1,0:T(8,128)(2,1)} %dy_ref.1, s32[128,1]{1,0:T(8,128)} %copy.8.slot_ref, f32[128,1]{1,0:T(8,128)} %copy.9.gate_ref, bf16[1024,384]{1,0:T(8,128)(2,1)} %bitcast.2, bf16[192,1024]{1,0:T(8,128)(2,1)} %bitcast.3), custom_call_target="tpu_custom_call" | custom-call | flops 704643072 | bytes 4718592 | tf_op jit(solution)/shard_map/routed_backward/pallas_call | solution.py:298
  57.3 0.0 copy-start
  57.3 2.4 %copy.12 = bf16[128,4096]{1,0:T(8,128)(2,1)} copy(bf16[128,4096]{1,0:T(8,128)(2,1)} %get-tuple-element.4) | data formatting | bytes 2097152
  59.7 0.0 copy-done
  59.7 0.9 %copy.13 = bf16[1,1024,384]{2,1,0:T(8,128)(2,1)} copy(bf16[1,1024,384]{2,1,0:T(8,128)(2,1)S(1)} %copy-done) | data formatting | bytes 1572864
Async XLA Ops:
  0.6 0.7 %copy-start.1 = (s32[128,1]{0,1:T(1,128)S(1)}, s32[128,1]{0,1:T(1,128)}, u32[]{:S(2)}) copy-start(s32[128,1]{0,1:T(1,128)} %param.8) | copy-start | bytes 1540
  1.3 0.7 %copy-start.2 = (f32[128,1]{0,1:T(1,128)S(1)}, f32[128,1]{0,1:T(1,128)}, u32[]{:S(2)}) copy-start(f32[128,1]{0,1:T(1,128)} %param.9) | copy-start | bytes 1540
  57.3 2.4 %copy-start = (bf16[1,1024,384]{2,1,0:T(8,128)(2,1)S(1)}, bf16[1,1024,384]{2,1,0:T(8,128)(2,1)}, u32[]{:S(2)}) copy-start(bf16[1,1024,384]{2,1,0:T(8,128)(2,1)} %get-tuple-element.5) | copy-start | bytes 2359300

commit v2 on v1

v2 whole, which is shorter than its diff:
```python
import functools

import jax
import jax.numpy as jnp
from jax import lax
from jax.experimental import pallas as pl
from jax.experimental.pallas import tpu as pltpu
from jax.sharding import PartitionSpec as P

GROUP = 8
CAP = 8
MESH = pl.DeviceIdType.MESH
F32 = jnp.float32
BF16 = jnp.bfloat16
NT = (((1,), (1,)), ((), ()))
TN = (((0,), (0,)), ((), ()))


def kernel(
    n_dp, windows,
    tok_ref, dy_ref, slot_ref, gate_ref, gu_ref, down_ref,
    fin_ref, gw_ref,
    pick, buf, xall, part, prcv, dgrcv, dguall, dxs, ret, back, fin, gut, downt,
    s_pick, r_pick, s_ag, r_ag, s_rs, r_rs, s_dg, r_dg, s_ret, r_ret, s_fin, r_fin,
):
    S = GROUP
    Z = S // 2
    W = windows
    n_same = n_dp * W
    tokens, width = tok_ref.shape
    cols = width // n_dp
    hidden = down_ref.shape[0]
    rows = n_dp * W * CAP
    me_d = lax.axis_index("dp")
    me_x = lax.axis_index("expert")
    me_w = me_x // S
    me_s = me_x % S
    zz = me_s // 2
    yy = me_s % 2

    def member(z, y):
        return (me_d, me_w * S + z * 2 + y)

    barrier = pltpu.get_barrier_semaphore()

    def same(k):
        flat = (me_d * W + me_w + k) % n_same
        return flat // W, flat % W

    def other(k):
        s = (me_s + k) % S
        return s // 2, s % 2

    for k in range(1, n_same):
        d, w = same(k)
        pl.semaphore_signal(barrier, inc=1, device_id=(d, w * S + me_s), device_id_type=MESH)
    for k in range(1, S):
        pl.semaphore_signal(barrier, inc=1, device_id=member(*other(k)), device_id_type=MESH)

    place = lax.broadcasted_iota(jnp.int32, (CAP, tokens), 0)
    for e in range(W):
        hit = slot_ref[e : e + 1, :] == place
        sel = jnp.where(hit, 1.0, 0.0).astype(BF16)
        weight = jnp.sum(jnp.where(hit, gate_ref[e : e + 1, :], 0.0), axis=1, keepdims=True)
        for d in range(n_dp):
            cut = slice(d * cols, (d + 1) * cols)
            x = jnp.dot(sel, tok_ref[:, cut], preferred_element_type=F32)
            g = jnp.dot(sel, dy_ref[:, cut], preferred_element_type=F32) * weight
            pick[d, e] = jnp.concatenate([x, g], axis=0).astype(BF16)
    pl.semaphore_wait(barrier, n_same - 1 + S - 1)

    def pick_copy(d, w):
        return pltpu.make_async_remote_copy(
            src_ref=pick.at[d, w], dst_ref=buf.at[zz, yy, me_d, me_w],
            send_sem=s_pick.at[d, w], recv_sem=r_pick.at[me_d, me_w],
            device_id=(d, w * S + me_s), device_id_type=MESH,
        )

    def pick_arrival(d, w):
        return pltpu.make_async_remote_copy(
            src_ref=pick.at[d, w], dst_ref=buf.at[zz, yy, d, w],
            send_sem=s_pick.at[d, w], recv_sem=r_pick.at[d, w],
            device_id=(d, w * S + me_s), device_id_type=MESH,
        )

    for k in range(1, n_same):
        pick_copy(*same(k)).start()
    buf[zz, yy, me_d, me_w] = pick[me_d, me_w]
    downt[...] = down_ref[...].T
    for k in range(1, n_same):
        pick_arrival(*same(k)).wait_recv()

    def spread(z, y, way, target):
        return pltpu.make_async_remote_copy(
            src_ref=buf.at[z, y], dst_ref=buf.at[z, y],
            send_sem=s_ag.at[z, way], recv_sem=r_ag.at[z, y],
            device_id=member(*target), device_id_type=MESH,
        )

    def reduce_copy(z, d, owner):
        return pltpu.make_async_remote_copy(
            src_ref=part.at[z, d], dst_ref=prcv.at[z, owner],
            send_sem=s_rs.at[z, d], recv_sem=r_rs.at[z, owner],
            device_id=(d, me_x), device_id_type=MESH,
        )

    def share_copy(z, d, owner):
        return pltpu.make_async_remote_copy(
            src_ref=dgrcv.at[z, me_d], dst_ref=dgrcv.at[z, owner],
            send_sem=s_dg.at[z, d], recv_sem=r_dg.at[z, owner],
            device_id=(d, me_x), device_id_type=MESH,
        )

    def return_copy(z, y, owner_z, owner_y):
        return pltpu.make_async_remote_copy(
            src_ref=dxs.at[z, y], dst_ref=ret.at[owner_z, owner_y],
            send_sem=s_ret.at[z, y], recv_sem=r_ret.at[owner_z, owner_y],
            device_id=member(z, y), device_id_type=MESH,
        )

    near = jnp.minimum(zz, Z - 1 - zz)

    def nth(m):
        alternating = ((m + 1) // 2) * (1 - 2 * (m % 2))
        far = m - near
        beyond = jnp.where(zz > Z - 1 - zz, -far, far)
        return zz + jnp.where(m <= 2 * near, alternating, beyond)

    def forward(z, act):
        @pl.when((z <= zz) & (zz + 1 < Z))
        def _():
            act(spread(z, yy, 0, (zz + 1, yy)))

        @pl.when((z >= zz) & (zz >= 1))
        def _():
            act(spread(z, yy, 1, (zz - 1, yy)))

        act(spread(z, yy, 2, (zz, 1 - yy)))

    def start(copy):
        copy.start()

    def pass_on(k):
        @pl.when(zz - k >= 0)
        def _():
            spread(zz - k, yy, 2, (zz, 1 - yy)).wait_recv()
            forward(zz - k, start)

        @pl.when(zz + k < Z)
        def _():
            spread(zz + k, yy, 2, (zz, 1 - yy)).wait_recv()
            forward(zz + k, start)

    def arrive(m):
        z = nth(m)
        spread(z, 1 - yy, 2, (zz, 1 - yy)).wait_recv()
        both = buf[z].astype(F32).reshape(2 * n_dp * W, 2, CAP, cols)
        x = both[:, 0].reshape(2 * rows, cols).astype(BF16)
        g = both[:, 1].reshape(2 * rows, cols).astype(BF16)
        xall[z] = x
        a_u = jnp.dot(x, gu_ref[...], preferred_element_type=F32)
        a_u = a_u.reshape(2, n_dp, W * CAP, 2 * hidden)
        dh = jnp.dot(g, downt[...], preferred_element_type=F32)
        dh = dh.reshape(2, n_dp, W * CAP, hidden)
        part[z, :, :, : 2 * hidden] = jnp.concatenate([a_u[0], a_u[1]], axis=1).astype(BF16)
        part[z, :, :, 2 * hidden :] = jnp.concatenate([dh[0], dh[1]], axis=1).astype(BF16)
        for k in range(1, n_dp):
            reduce_copy(z, (me_d + k) % n_dp, me_d).start()

    def activate(m):
        z = nth(m)
        total = part[z, me_d].astype(F32)
        for k in range(1, n_dp):
            d = (me_d + k) % n_dp
            reduce_copy(z, d, d).wait_recv()
            total = total + prcv[z, d].astype(F32)
        pre = total[:, :hidden]
        up_part = total[:, hidden : 2 * hidden]
        dh = total[:, 2 * hidden :]
        sig = jax.nn.sigmoid(pre)
        dgate = dh * up_part * sig * (1.0 + pre * (1.0 - sig))
        dup = dh * (pre * sig)
        dgrcv[z, me_d] = jnp.concatenate(
            [dgate.reshape(2 * W, CAP, hidden), dup.reshape(2 * W, CAP, hidden)], axis=1
        ).astype(BF16)
        for k in range(1, n_dp):
            share_copy(z, (me_d + k) % n_dp, me_d).start()

    def give_back(m):
        z = nth(m)
        for k in range(1, n_dp):
            d = (me_d + k) % n_dp
            share_copy(z, d, d).wait_recv()
        both = dgrcv[z].astype(F32).reshape(n_dp, 2, W, 2, CAP, hidden)
        dgate = jnp.concatenate([both[:, y, :, 0].reshape(rows, hidden) for y in range(2)], axis=0)
        dup = jnp.concatenate([both[:, y, :, 1].reshape(rows, hidden) for y in range(2)], axis=0)
        dgu = jnp.concatenate([dgate, dup], axis=1).astype(BF16)
        dguall[z] = dgu
        dx = jnp.dot(dgu, gut[...], preferred_element_type=F32).astype(BF16)
        dxs[z] = dx.reshape(2, rows, cols)
        return_copy(z, 1 - yy, zz, yy).start()

        @pl.when(m > 0)
        def _():
            return_copy(z, yy, zz, yy).start()

    def step(m, carry):
        @pl.when(m < Z)
        def _():
            pass_on(m + 1)
            arrive(m)

        @pl.when((m >= 1) & (m < Z + 1))
        def _():
            activate(m - 1)

        @pl.when(m >= 2)
        def _():
            give_back(m - 2)

        return carry

    forward(zz, start)
    gut[...] = gu_ref[...].T
    lax.fori_loop(0, Z + 2, step, 0)

    gw_ref[0] = lax.dot_general(
        xall[...].reshape(S * rows, cols), dguall[...].reshape(S * rows, 2 * hidden), TN,
        preferred_element_type=F32,
    ).astype(BF16)

    total = dxs[zz, yy].astype(F32)
    for k in range(1, S):
        z, y = other(k)
        return_copy(z, y, z, y).wait_recv()
        total = total + ret[z, y].astype(F32)
    total = total.reshape(n_dp, W, CAP, cols)
    back[...] = jnp.concatenate(
        [total[..., : cols // 2], total[..., cols // 2 :]], axis=2
    ).astype(BF16)

    def fin_copy(d, w, owner_d, owner_w):
        return pltpu.make_async_remote_copy(
            src_ref=back.at[d, w], dst_ref=fin.at[owner_d, owner_w],
            send_sem=s_fin.at[d, w], recv_sem=r_fin.at[owner_d, owner_w],
            device_id=(d, w * S + me_s), device_id_type=MESH,
        )

    for k in range(1, n_same):
        d, w = same(k)
        fin_copy(d, w, me_d, me_w).start()
    fin[me_d, me_w] = back[me_d, me_w]

    for k in range(1, n_same):
        pick_copy(*same(k)).wait_send()
    for k in range(1, S):
        z, y = other(k)
        return_copy(z, y, zz, yy).wait_send()

    def wait_send(copy):
        copy.wait_send()

    def drain(z, carry):
        forward(z, wait_send)
        for k in range(1, n_dp):
            d = (me_d + k) % n_dp
            reduce_copy(z, d, me_d).wait_send()
            share_copy(z, d, me_d).wait_send()
        return carry

    lax.fori_loop(0, Z, drain, 0)
    for k in range(1, n_same):
        d, w = same(k)
        fin_copy(d, w, d, w).wait_recv()
        fin_copy(d, w, me_d, me_w).wait_send()
    fin_ref[...] = fin[...]


def place_rows(fin_ref, slot_ref, gx_ref):
    n_dp, W, _, half = fin_ref.shape
    tokens = gx_ref.shape[0]
    place = lax.broadcasted_iota(jnp.int32, (2 * CAP, tokens), 0)
    for h in range(2):
        hits = []
        for e in range(W):
            hit = (slot_ref[e : e + 1, :] == place - h * CAP) & (place >= h * CAP)
            hits.append(jnp.where(hit, 1.0, 0.0).T.astype(BF16))
        for d in range(n_dp):
            out = jnp.dot(hits[0], fin_ref[d, 0], preferred_element_type=F32)
            for e in range(1, W):
                out = out + jnp.dot(hits[e], fin_ref[d, e], preferred_element_type=F32)
            at = (2 * d + h) * half
            gx_ref[:, at : at + half] = out.astype(BF16)


def on_device(n_dp, tokens, output_gradient, slot, gate_weight, gate_up_weight, down_weight):
    W = slot.shape[1]
    S = GROUP
    Z = S // 2
    _, cols, wide = gate_up_weight.shape
    hidden = wide // 2
    rows = n_dp * W * CAP
    vmem = pl.BlockSpec(memory_space=pltpu.VMEM)
    dma = pltpu.SemaphoreType.DMA
    slot_row = slot.T
    fin, grad_gate_up = pl.pallas_call(
        functools.partial(kernel, n_dp, W),
        out_shape=(
            jax.ShapeDtypeStruct((n_dp, W, 2 * CAP, cols // 2), BF16),
            jax.ShapeDtypeStruct(gate_up_weight.shape, BF16),
        ),
        in_specs=[vmem] * 6,
        out_specs=(vmem, vmem),
        scratch_shapes=[
            pltpu.VMEM((n_dp, W, 2 * CAP, cols), BF16),
            pltpu.VMEM((Z, 2, n_dp, W, 2 * CAP, cols), BF16),
            pltpu.VMEM((Z, 2 * rows, cols), BF16),
            pltpu.VMEM((Z, n_dp, 2 * W * CAP, 3 * hidden), BF16),
            pltpu.VMEM((Z, n_dp, 2 * W * CAP, 3 * hidden), BF16),
            pltpu.VMEM((Z, n_dp, 2 * W, 2 * CAP, hidden), BF16),
            pltpu.VMEM((Z, 2 * rows, wide), BF16),
            pltpu.VMEM((Z, 2, rows, cols), BF16),
            pltpu.VMEM((Z, 2, rows, cols), BF16),
            pltpu.VMEM((n_dp, W, 2 * CAP, cols // 2), BF16),
            pltpu.VMEM((n_dp, W, 2 * CAP, cols // 2), BF16),
            pltpu.VMEM((wide, cols), BF16),
            pltpu.VMEM((cols, hidden), BF16),
            dma((n_dp, W)), dma((n_dp, W)),
            dma((Z, 3)), dma((Z, 2)),
            dma((Z, n_dp)), dma((Z, n_dp)),
            dma((Z, n_dp)), dma((Z, n_dp)),
            dma((Z, 2)), dma((Z, 2)),
            dma((n_dp, W)), dma((n_dp, W)),
        ],
        compiler_params=pltpu.CompilerParams(
            collective_id=0, has_side_effects=True, vmem_limit_bytes=58 * 1024 * 1024
        ),
        cost_estimate=pl.CostEstimate(
            flops=14 * S * rows * cols * hidden,
            bytes_accessed=4 * tokens.size + 4 * gate_up_weight.size, transcendentals=0,
        ),
        name="routed_backward",
    )(tokens, output_gradient, slot_row, gate_weight.T, gate_up_weight[0], down_weight[0])
    grad_tokens = pl.pallas_call(
        place_rows,
        out_shape=jax.ShapeDtypeStruct(tokens.shape, BF16),
        in_specs=[vmem] * 2,
        out_specs=vmem,
        compiler_params=pltpu.CompilerParams(vmem_limit_bytes=32 * 1024 * 1024),
        name="place_rows",
    )(fin, slot_row)
    return grad_tokens, grad_gate_up


def solution(mesh):
    in_specs = (
        P(("dp", "expert"), None),
        P(("dp", "expert"), None),
        P(("dp", "expert"), None),
        P(("dp", "expert"), None),
        P("expert", "dp", None),
        P("expert", None, "dp"),
    )
    out_specs = (P(("dp", "expert"), None), P("expert", "dp", None))
    return jax.shard_map(
        functools.partial(on_device, mesh.shape["dp"]),
        mesh=mesh, in_specs=in_specs, out_specs=out_specs, check_vma=False,
    )
```

time: 60.7 us -> 51.4 us (0.85)
  Pallas kernels: 54.5 us -> 48.2 us
  local copies, waits for them, and re-layouts: 5.38 us -> 2.37 us
    pallas_call x1, Pallas kernels: 54.5 us -> 46.8 us  [on_device(): pl.pallas_call(functools.partial(kernel, n_dp, W), out_shape=(jax.ShapeDt...]
    unnamed x10 -> x7, local copies, waits for them, and re-layouts: 5.38 us -> 2.37 us
    pallas_call x0 -> x1, Pallas kernels: none -> 1.44 us  [on_device(): pl.pallas_call(place_rows, out_shape=jax.ShapeDtypeStruct(tokens.shape, B...]
where the time goes in v2:
time: 51.4 us; the launch traced here: 51.2 us
  Pallas kernels  48.2 us (94%)
  local copies, waits for them, and re-layouts  2.37 us (5%)
  between operations  0.65 us (1%)
    pallas_call x1, Pallas kernels, on_device(): pl.pallas_call(functools.partial(kernel, n_dp, W), out_shape=(jax.ShapeDt...  46.8 us
    unnamed x7, local copies, waits for them, and re-layouts  2.37 us
    pallas_call x1, Pallas kernels, on_device(): pl.pallas_call(place_rows, out_shape=jax.ShapeDtypeStruct(tokens.shape, B...  1.44 us

profile of v2, /device:TPU:0, one launch (start us, length us, event | category | flops | bytes accessed | tf_op | source)
XLA Modules:
  0.0 51.2 jit_solution(17118486330393674188)
XLA Ops:
  0.6 46.8 %routed_backward.1 = (bf16[4,1,16,512]{3,2,1,0:T(8,128)(2,1)}, bf16[1,1024,384]{2,1,0:T(8,128)(2,1)}) custom-call(bf16[128,4096]{1,0:T(8,128)(2,1)} %tok_ref.1, bf16[128,4096]{1,0:T(8,128)(2,1)} %dy_ref.1, s32[1,128]{1,0:T(1,128)} %bitcast.4, f32[1,128]{1,0:T(1,128)} %bitcast.8, bf16[1024,384]{1,0:T(8,128)(2,1)} %bitcast.6, bf16[192,1024]{1,0:T(8,128)(2,1)} %bitcast.7), custom_call_target="tpu_custom_call" | custom-call | flops 704643072 | bytes 3670016 | tf_op jit(solution)/shard_map/routed_backward/pallas_call | solution.py:306
  47.4 0.0 copy-start.1
  47.4 0.6 %copy-done.1 = s32[128,1]{0,1:T(1,128)S(1)} copy-done((s32[128,1]{0,1:T(1,128)S(1)}, s32[128,1]{0,1:T(1,128)}, u32[]{:S(2)}) %copy-start.1) | copy-done | bytes 536
  48.1 0.0 copy-start
  48.1 0.8 %copy-done = bf16[4,1,16,512]{3,2,1,0:T(8,128)(2,1)S(1)} copy-done((bf16[4,1,16,512]{3,2,1,0:T(8,128)(2,1)S(1)}, bf16[4,1,16,512]{3,2,1,0:T(8,128)(2,1)}, u32[]{:S(2)}) %copy-start) | copy-done | bytes 65560
  48.9 0.0 copy-start.2
  48.9 1.4 %place_rows.1 = bf16[128,4096]{1,0:T(8,128)(2,1)} custom-call(bf16[4,1,16,512]{3,2,1,0:T(8,128)(2,1)S(1)} %copy-done, s32[1,128]{1,0:T(1,128)S(1)} %bitcast.5), custom_call_target="tpu_custom_call" | custom-call | tf_op jit(solution)/shard_map/place_rows/pallas_call | solution.py:344
  50.4 0.0 copy-done.2
  50.4 0.9 %copy.9 = bf16[1,1024,384]{2,1,0:T(8,128)(2,1)} copy(bf16[1,1024,384]{2,1,0:T(8,128)(2,1)S(1)} %copy-done.2) | data formatting | bytes 1572864
Async XLA Ops:
  47.4 0.7 %copy-start.1 = (s32[128,1]{0,1:T(1,128)S(1)}, s32[128,1]{0,1:T(1,128)}, u32[]{:S(2)}) copy-start(s32[128,1]{0,1:T(1,128)} %param.8) | copy-start | bytes 1540
  48.1 0.8 %copy-start = (bf16[4,1,16,512]{3,2,1,0:T(8,128)(2,1)S(1)}, bf16[4,1,16,512]{3,2,1,0:T(8,128)(2,1)}, u32[]{:S(2)}) copy-start(bf16[4,1,16,512]{3,2,1,0:T(8,128)(2,1)} %get-tuple-element.4.fin_ref) | copy-start | bytes 196612
  48.9 1.4 %copy-start.2 = (bf16[1,1024,384]{2,1,0:T(8,128)(2,1)S(1)}, bf16[1,1024,384]{2,1,0:T(8,128)(2,1)}, u32[]{:S(2)}) copy-start(bf16[1,1024,384]{2,1,0:T(8,128)(2,1)} %get-tuple-element.9) | copy-start | bytes 2359300

commit v3 on v2

--- a/solution.py
+++ b/solution.py
@@ -29,6 +29,7 @@
     n_same = n_dp * W
     tokens, width = tok_ref.shape
     cols = width // n_dp
+    half = cols // 2
     hidden = down_ref.shape[0]
     rows = n_dp * W * CAP
     me_d = lax.axis_index("dp")
@@ -57,43 +58,46 @@
     for k in range(1, S):
         pl.semaphore_signal(barrier, inc=1, device_id=member(*other(k)), device_id_type=MESH)
 
+    def pick_copy(h, d, w):
+        return pltpu.make_async_remote_copy(
+            src_ref=pick.at[h, d, w], dst_ref=buf.at[zz, yy, h, me_d, me_w],
+            send_sem=s_pick.at[h, d, w], recv_sem=r_pick.at[h, me_d, me_w],
+            device_id=(d, w * S + me_s), device_id_type=MESH,
+        )
+
+    def pick_arrival(h, d, w):
+        return pltpu.make_async_remote_copy(
+            src_ref=pick.at[h, d, w], dst_ref=buf.at[zz, yy, h, d, w],
+            send_sem=s_pick.at[h, d, w], recv_sem=r_pick.at[h, d, w],
+            device_id=(d, w * S + me_s), device_id_type=MESH,
+        )
+
     place = lax.broadcasted_iota(jnp.int32, (CAP, tokens), 0)
+    sels, weights = [], []
     for e in range(W):
         hit = slot_ref[e : e + 1, :] == place
-        sel = jnp.where(hit, 1.0, 0.0).astype(BF16)
-        weight = jnp.sum(jnp.where(hit, gate_ref[e : e + 1, :], 0.0), axis=1, keepdims=True)
-        for d in range(n_dp):
-            cut = slice(d * cols, (d + 1) * cols)
-            x = jnp.dot(sel, tok_ref[:, cut], preferred_element_type=F32)
-            g = jnp.dot(sel, dy_ref[:, cut], preferred_element_type=F32) * weight
-            pick[d, e] = jnp.concatenate([x, g], axis=0).astype(BF16)
-    pl.semaphore_wait(barrier, n_same - 1 + S - 1)
-
-    def pick_copy(d, w):
-        return pltpu.make_async_remote_copy(
-            src_ref=pick.at[d, w], dst_ref=buf.at[zz, yy, me_d, me_w],
-            send_sem=s_pick.at[d, w], recv_sem=r_pick.at[me_d, me_w],
-            device_id=(d, w * S + me_s), device_id_type=MESH,
-        )
-
-    def pick_arrival(d, w):
-        return pltpu.make_async_remote_copy(
-            src_ref=pick.at[d, w], dst_ref=buf.at[zz, yy, d, w],
-            send_sem=s_pick.at[d, w], recv_sem=r_pick.at[d, w],
-            device_id=(d, w * S + me_s), device_id_type=MESH,
-        )
-
-    for k in range(1, n_same):
-        pick_copy(*same(k)).start()
-    buf[zz, yy, me_d, me_w] = pick[me_d, me_w]
+        sels.append(jnp.where(hit, 1.0, 0.0).astype(BF16))
+        weights.append(
+            jnp.sum(jnp.where(hit, gate_ref[e : e + 1, :], 0.0), axis=1, keepdims=True)
+        )
+    for h in range(2):
+        for e in range(W):
+            for d in range(n_dp):
+                cut = slice(d * cols + h * half, d * cols + (h + 1) * half)
+                x = jnp.dot(sels[e], tok_ref[:, cut], preferred_element_type=F32)
+                g = jnp.dot(sels[e], dy_ref[:, cut], preferred_element_type=F32) * weights[e]
+                pick[h, d, e] = jnp.concatenate([x, g], axis=0).astype(BF16)
+        if h == 0:
+            pl.semaphore_wait(barrier, n_same - 1 + S - 1)
+        for k in range(1, n_same):
+            pick_copy(h, *same(k)).start()
+        buf[zz, yy, h, me_d, me_w] = pick[h, me_d, me_w]
     downt[...] = down_ref[...].T
-    for k in range(1, n_same):
-        pick_arrival(*same(k)).wait_recv()
-
-    def spread(z, y, way, target):
-        return pltpu.make_async_remote_copy(
-            src_ref=buf.at[z, y], dst_ref=buf.at[z, y],
-            send_sem=s_ag.at[z, way], recv_sem=r_ag.at[z, y],
+
+    def spread(z, y, h, way, target):
+        return pltpu.make_async_remote_copy(
+            src_ref=buf.at[z, y, h], dst_ref=buf.at[z, y, h],
+            send_sem=s_ag.at[z, h, way], recv_sem=r_ag.at[z, y, h],
             device_id=member(*target), device_id_type=MESH,
         )
 
@@ -126,41 +130,44 @@
         beyond = jnp.where(zz > Z - 1 - zz, -far, far)
         return zz + jnp.where(m <= 2 * near, alternating, beyond)
 
-    def forward(z, act):
+    def forward(z, h, act):
         @pl.when((z <= zz) & (zz + 1 < Z))
         def _():
-            act(spread(z, yy, 0, (zz + 1, yy)))
+            act(spread(z, yy, h, 0, (zz + 1, yy)))
 
         @pl.when((z >= zz) & (zz >= 1))
         def _():
-            act(spread(z, yy, 1, (zz - 1, yy)))
-
-        act(spread(z, yy, 2, (zz, 1 - yy)))
+            act(spread(z, yy, h, 1, (zz - 1, yy)))
+
+        act(spread(z, yy, h, 2, (zz, 1 - yy)))
 
     def start(copy):
         copy.start()
 
-    def pass_on(k):
+    def pass_on(k, h):
         @pl.when(zz - k >= 0)
         def _():
-            spread(zz - k, yy, 2, (zz, 1 - yy)).wait_recv()
-            forward(zz - k, start)
+            spread(zz - k, yy, h, 2, (zz, 1 - yy)).wait_recv()
+            forward(zz - k, h, start)
 
         @pl.when(zz + k < Z)
         def _():
-            spread(zz + k, yy, 2, (zz, 1 - yy)).wait_recv()
-            forward(zz + k, start)
+            spread(zz + k, yy, h, 2, (zz, 1 - yy)).wait_recv()
+            forward(zz + k, h, start)
 
     def arrive(m):
         z = nth(m)
-        spread(z, 1 - yy, 2, (zz, 1 - yy)).wait_recv()
-        both = buf[z].astype(F32).reshape(2 * n_dp * W, 2, CAP, cols)
-        x = both[:, 0].reshape(2 * rows, cols).astype(BF16)
-        g = both[:, 1].reshape(2 * rows, cols).astype(BF16)
-        xall[z] = x
-        a_u = jnp.dot(x, gu_ref[...], preferred_element_type=F32)
+        a_u = dh = 0.0
+        for h in range(2):
+            spread(z, 1 - yy, h, 2, (zz, 1 - yy)).wait_recv()
+            both = buf[z, :, h].astype(F32).reshape(2 * n_dp * W, 2, CAP, half)
+            x = both[:, 0].reshape(2 * rows, half).astype(BF16)
+            g = both[:, 1].reshape(2 * rows, half).astype(BF16)
+            cut = slice(h * half, (h + 1) * half)
+            xall[z, :, cut] = x
+            a_u = a_u + jnp.dot(x, gu_ref[cut], preferred_element_type=F32)
+            dh = dh + jnp.dot(g, downt[cut], preferred_element_type=F32)
         a_u = a_u.reshape(2, n_dp, W * CAP, 2 * hidden)
-        dh = jnp.dot(g, downt[...], preferred_element_type=F32)
         dh = dh.reshape(2, n_dp, W * CAP, hidden)
         part[z, :, :, : 2 * hidden] = jnp.concatenate([a_u[0], a_u[1]], axis=1).astype(BF16)
         part[z, :, :, 2 * hidden :] = jnp.concatenate([dh[0], dh[1]], axis=1).astype(BF16)
@@ -207,8 +214,9 @@
     def step(m, carry):
         @pl.when(m < Z)
         def _():
-            pass_on(m + 1)
+            pass_on(m + 1, 1)
             arrive(m)
+            pass_on(m + 2, 0)
 
         @pl.when((m >= 1) & (m < Z + 1))
         def _():
@@ -220,8 +228,12 @@
 
         return carry
 
-    forward(zz, start)
+    for h in range(2):
+        for k in range(1, n_same):
+            pick_arrival(h, *same(k)).wait_recv()
+        forward(zz, h, start)
     gut[...] = gu_ref[...].T
+    pass_on(1, 0)
     lax.fori_loop(0, Z + 2, step, 0)
 
     gw_ref[0] = lax.dot_general(
@@ -252,7 +264,8 @@
     fin[me_d, me_w] = back[me_d, me_w]
 
     for k in range(1, n_same):
-        pick_copy(*same(k)).wait_send()
+        for h in range(2):
+            pick_copy(h, *same(k)).wait_send()
     for k in range(1, S):
         z, y = other(k)
         return_copy(z, y, zz, yy).wait_send()
@@ -261,7 +274,8 @@
         copy.wait_send()
 
     def drain(z, carry):
-        forward(z, wait_send)
+        for h in range(2):
+            forward(z, h, wait_send)
         for k in range(1, n_dp):
             d = (me_d + k) % n_dp
             reduce_copy(z, d, me_d).wait_send()
@@ -276,9 +290,18 @@
     fin_ref[...] = fin[...]
 
 
-def place_rows(fin_ref, slot_ref, gx_ref):
+def place_rows(fin_hbm, slot_hbm, gw_hbm, gx_ref, gw_ref, fin_ref, slot_ref, sems):
     n_dp, W, _, half = fin_ref.shape
     tokens = gx_ref.shape[0]
+    copies = [
+        pltpu.make_async_copy(slot_hbm, slot_ref, sems.at[0]),
+        pltpu.make_async_copy(fin_hbm, fin_ref, sems.at[1]),
+        pltpu.make_async_copy(gw_hbm, gw_ref, sems.at[2]),
+    ]
+    for copy in copies:
+        copy.start()
+    copies[0].wait()
+    copies[1].wait()
     place = lax.broadcasted_iota(jnp.int32, (2 * CAP, tokens), 0)
     for h in range(2):
         hits = []
@@ -291,6 +314,7 @@
                 out = out + jnp.dot(hits[e], fin_ref[d, e], preferred_element_type=F32)
             at = (2 * d + h) * half
             gx_ref[:, at : at + half] = out.astype(BF16)
+    copies[2].wait()
 
 
 def on_device(n_dp, tokens, output_gradient, slot, gate_weight, gate_up_weight, down_weight):
@@ -312,8 +336,8 @@
         in_specs=[vmem] * 6,
         out_specs=(vmem, vmem),
         scratch_shapes=[
-            pltpu.VMEM((n_dp, W, 2 * CAP, cols), BF16),
-            pltpu.VMEM((Z, 2, n_dp, W, 2 * CAP, cols), BF16),
+            pltpu.VMEM((2, n_dp, W, 2 * CAP, cols // 2), BF16),
+            pltpu.VMEM((Z, 2, 2, n_dp, W, 2 * CAP, cols // 2), BF16),
             pltpu.VMEM((Z, 2 * rows, cols), BF16),
             pltpu.VMEM((Z, n_dp, 2 * W * CAP, 3 * hidden), BF16),
             pltpu.VMEM((Z, n_dp, 2 * W * CAP, 3 * hidden), BF16),
@@ -325,8 +349,8 @@
             pltpu.VMEM((n_dp, W, 2 * CAP, cols // 2), BF16),
             pltpu.VMEM((wide, cols), BF16),
             pltpu.VMEM((cols, hidden), BF16),
-            dma((n_dp, W)), dma((n_dp, W)),
-            dma((Z, 3)), dma((Z, 2)),
+            dma((2, n_dp, W)), dma((2, n_dp, W)),
+            dma((Z, 2, 3)), dma((Z, 2, 2)),
             dma((Z, n_dp)), dma((Z, n_dp)),
             dma((Z, n_dp)), dma((Z, n_dp)),
             dma((Z, 2)), dma((Z, 2)),
@@ -341,15 +365,23 @@
         ),
         name="routed_backward",
     )(tokens, output_gradient, slot_row, gate_weight.T, gate_up_weight[0], down_weight[0])
-    grad_tokens = pl.pallas_call(
+    anywhere = pl.BlockSpec(memory_space=pl.ANY)
+    return pl.pallas_call(
         place_rows,
-        out_shape=jax.ShapeDtypeStruct(tokens.shape, BF16),
-        in_specs=[vmem] * 2,
-        out_specs=vmem,
-        compiler_params=pltpu.CompilerParams(vmem_limit_bytes=32 * 1024 * 1024),
+        out_shape=(
+            jax.ShapeDtypeStruct(tokens.shape, BF16),
+            jax.ShapeDtypeStruct(gate_up_weight.shape, BF16),
+        ),
+        in_specs=[anywhere] * 3,
+        out_specs=(vmem, vmem),
+        scratch_shapes=[
+            pltpu.VMEM(fin.shape, BF16),
+            pltpu.VMEM(slot_row.shape, jnp.int32),
+            dma((3,)),
+        ],
+        compiler_params=pltpu.CompilerParams(vmem_limit_bytes=58 * 1024 * 1024),
         name="place_rows",
-    )(fin, slot_row)
-    return grad_tokens, grad_gate_up
+    )(fin, slot_row, grad_gate_up)
 
 
 def solution(mesh):

time: 51.4 us -> 49.1 us (0.955)
  local copies, waits for them, and re-layouts: 2.37 us -> 0 us
    unnamed x7 -> x0, local copies, waits for them, and re-layouts: 2.37 us -> none
    pallas_call x1, Pallas kernels: 1.44 us -> 2.59 us  [on_device(): pl.pallas_call(place_rows, out_shape=(jax.ShapeDtypeStruct(tokens.shape,...]
    pallas_call x1, Pallas kernels: 46.8 us -> 45.7 us  [on_device(): pl.pallas_call(functools.partial(kernel, n_dp, W), out_shape=(jax.ShapeDt...]
where the time goes in v3:
time: 49.1 us; the launch traced here: 48.9 us
  Pallas kernels  48.3 us (98%)
  between operations  0.64 us (1%)
    pallas_call x1, Pallas kernels, on_device(): pl.pallas_call(functools.partial(kernel, n_dp, W), out_shape=(jax.ShapeDt...  45.7 us
    pallas_call x1, Pallas kernels, on_device(): pl.pallas_call(place_rows, out_shape=(jax.ShapeDtypeStruct(tokens.shape,...  2.59 us

profile of v3, /device:TPU:0, one launch (start us, length us, event | category | flops | bytes accessed | tf_op | source)
XLA Modules:
  0.0 48.9 jit_solution(1873898128793909674)
XLA Ops:
  0.6 45.7 %routed_backward.1 = (bf16[4,1,16,512]{3,2,1,0:T(8,128)(2,1)}, bf16[1,1024,384]{2,1,0:T(8,128)(2,1)}) custom-call(bf16[128,4096]{1,0:T(8,128)(2,1)} %tok_ref.1, bf16[128,4096]{1,0:T(8,128)(2,1)} %dy_ref.1, s32[1,128]{1,0:T(1,128)} %bitcast.6, f32[1,128]{1,0:T(1,128)} %bitcast.8, bf16[1024,384]{1,0:T(8,128)(2,1)} %bitcast.4, bf16[192,1024]{1,0:T(8,128)(2,1)} %bitcast.5), custom_call_target="tpu_custom_call" | custom-call | flops 704643072 | bytes 3670016 | tf_op jit(solution)/shard_map/routed_backward/pallas_call | solution.py:330
  46.3 2.6 %place_rows.1 = (bf16[128,4096]{1,0:T(8,128)(2,1)}, bf16[1,1024,384]{2,1,0:T(8,128)(2,1)}) custom-call(bf16[4,1,16,512]{3,2,1,0:T(8,128)(2,1)} %get-tuple-element.4.fin_hbm, s32[1,128]{1,0:T(1,128)} %bitcast.7, bf16[1,1024,384]{2,1,0:T(8,128)(2,1)} %get-tuple-element.5.gw_hbm), custom_call_target="tpu_custom_call" | custom-call | tf_op jit(solution)/shard_map/place_rows/pallas_call | solution.py:369

commit v4 on v3

--- a/solution.py
+++ b/solution.py
@@ -20,8 +20,8 @@
     n_dp, windows,
     tok_ref, dy_ref, slot_ref, gate_ref, gu_ref, down_ref,
     fin_ref, gw_ref,
-    pick, buf, xall, part, prcv, dgrcv, dguall, dxs, ret, back, fin, gut, downt,
-    s_pick, r_pick, s_ag, r_ag, s_rs, r_rs, s_dg, r_dg, s_ret, r_ret, s_fin, r_fin,
+    pick, buf, xall, part, prcv, dgrcv, dguall, dxs, across, sums, ret, back, fin, gut, downt,
+    s_pick, r_pick, s_ag, r_ag, s_rs, r_rs, s_dg, r_dg, s_cross, r_cross, s_ret, r_ret, s_fin, r_fin,
 ):
     S = GROUP
     Z = S // 2
@@ -115,11 +115,18 @@
             device_id=(d, me_x), device_id_type=MESH,
         )
 
-    def return_copy(z, y, owner_z, owner_y):
-        return pltpu.make_async_remote_copy(
-            src_ref=dxs.at[z, y], dst_ref=ret.at[owner_z, owner_y],
-            send_sem=s_ret.at[z, y], recv_sem=r_ret.at[owner_z, owner_y],
-            device_id=member(z, y), device_id_type=MESH,
+    def cross_copy(z):
+        return pltpu.make_async_remote_copy(
+            src_ref=dxs.at[z, 1 - yy], dst_ref=across.at[z],
+            send_sem=s_cross.at[z], recv_sem=r_cross.at[z],
+            device_id=member(zz, 1 - yy), device_id_type=MESH,
+        )
+
+    def return_copy(z, owner):
+        return pltpu.make_async_remote_copy(
+            src_ref=sums.at[z], dst_ref=ret.at[owner],
+            send_sem=s_ret.at[z], recv_sem=r_ret.at[owner],
+            device_id=member(z, yy), device_id_type=MESH,
         )
 
     near = jnp.minimum(zz, Z - 1 - zz)
@@ -205,11 +212,16 @@
         dguall[z] = dgu
         dx = jnp.dot(dgu, gut[...], preferred_element_type=F32).astype(BF16)
         dxs[z] = dx.reshape(2, rows, cols)
-        return_copy(z, 1 - yy, zz, yy).start()
+        cross_copy(z).start()
+
+    def combine(m):
+        z = nth(m)
+        cross_copy(z).wait_recv()
+        sums[z] = (dxs[z, yy].astype(F32) + across[z].astype(F32)).astype(BF16)
 
         @pl.when(m > 0)
         def _():
-            return_copy(z, yy, zz, yy).start()
+            return_copy(z, zz).start()
 
     def step(m, carry):
         @pl.when(m < Z)
@@ -225,6 +237,10 @@
         @pl.when(m >= 2)
         def _():
             give_back(m - 2)
+
+        @pl.when(m >= 3)
+        def _():
+            combine(m - 3)
 
         return carry
 
@@ -236,16 +252,22 @@
     pass_on(1, 0)
     lax.fori_loop(0, Z + 2, step, 0)
 
-    gw_ref[0] = lax.dot_general(
-        xall[...].reshape(S * rows, cols), dguall[...].reshape(S * rows, 2 * hidden), TN,
-        preferred_element_type=F32,
-    ).astype(BF16)
-
-    total = dxs[zz, yy].astype(F32)
-    for k in range(1, S):
-        z, y = other(k)
-        return_copy(z, y, z, y).wait_recv()
-        total = total + ret[z, y].astype(F32)
+    def weight_gradient(h):
+        cut = slice(h * half, (h + 1) * half)
+        gw_ref[0, cut] = lax.dot_general(
+            xall[:, :, cut].reshape(S * rows, half), dguall[...].reshape(S * rows, 2 * hidden), TN,
+            preferred_element_type=F32,
+        ).astype(BF16)
+
+    weight_gradient(0)
+    combine(Z - 1)
+    weight_gradient(1)
+
+    total = sums[zz].astype(F32)
+    for k in range(1, Z):
+        z = (zz + k) % Z
+        return_copy(z, z).wait_recv()
+        total = total + ret[z].astype(F32)
     total = total.reshape(n_dp, W, CAP, cols)
     back[...] = jnp.concatenate(
         [total[..., : cols // 2], total[..., cols // 2 :]], axis=2
@@ -266,9 +288,8 @@
     for k in range(1, n_same):
         for h in range(2):
             pick_copy(h, *same(k)).wait_send()
-    for k in range(1, S):
-        z, y = other(k)
-        return_copy(z, y, zz, yy).wait_send()
+    for k in range(1, Z):
+        return_copy((zz + k) % Z, zz).wait_send()
 
     def wait_send(copy):
         copy.wait_send()
@@ -276,6 +297,7 @@
     def drain(z, carry):
         for h in range(2):
             forward(z, h, wait_send)
+        cross_copy(z).wait_send()
         for k in range(1, n_dp):
             d = (me_d + k) % n_dp
             reduce_copy(z, d, me_d).wait_send()
@@ -344,7 +366,9 @@
             pltpu.VMEM((Z, n_dp, 2 * W, 2 * CAP, hidden), BF16),
             pltpu.VMEM((Z, 2 * rows, wide), BF16),
             pltpu.VMEM((Z, 2, rows, cols), BF16),
-            pltpu.VMEM((Z, 2, rows, cols), BF16),
+            pltpu.VMEM((Z, rows, cols), BF16),
+            pltpu.VMEM((Z, rows, cols), BF16),
+            pltpu.VMEM((Z, rows, cols), BF16),
             pltpu.VMEM((n_dp, W, 2 * CAP, cols // 2), BF16),
             pltpu.VMEM((n_dp, W, 2 * CAP, cols // 2), BF16),
             pltpu.VMEM((wide, cols), BF16),
@@ -353,7 +377,8 @@
             dma((Z, 2, 3)), dma((Z, 2, 2)),
             dma((Z, n_dp)), dma((Z, n_dp)),
             dma((Z, n_dp)), dma((Z, n_dp)),
-            dma((Z, 2)), dma((Z, 2)),
+            dma((Z,)), dma((Z,)),
+            dma((Z,)), dma((Z,)),
             dma((n_dp, W)), dma((n_dp, W)),
         ],
         compiler_params=pltpu.CompilerParams(

time: 49.1 us -> 48.7 us (level)
  no operation moved by 1% of the time
where the time goes in v4:
time: 48.7 us; the launch traced here: 48.5 us
  Pallas kernels  47.9 us (98%)
  between operations  0.64 us (1%)
    pallas_call x1, Pallas kernels, on_device(): pl.pallas_call(functools.partial(kernel, n_dp, W), out_shape=(jax.ShapeDt...  45.3 us
    pallas_call x1, Pallas kernels, on_device(): pl.pallas_call(place_rows, out_shape=(jax.ShapeDtypeStruct(tokens.shape,...  2.59 us

profile of v4, /device:TPU:0, one launch (start us, length us, event | category | flops | bytes accessed | tf_op | source)
XLA Modules:
  0.0 48.5 jit_solution(16181052090400976234)
XLA Ops:
  0.6 45.3 %routed_backward.1 = (bf16[4,1,16,512]{3,2,1,0:T(8,128)(2,1)}, bf16[1,1024,384]{2,1,0:T(8,128)(2,1)}) custom-call(bf16[128,4096]{1,0:T(8,128)(2,1)} %tok_ref.1, bf16[128,4096]{1,0:T(8,128)(2,1)} %dy_ref.1, s32[1,128]{1,0:T(1,128)} %bitcast.6, f32[1,128]{1,0:T(1,128)} %bitcast.8, bf16[1024,384]{1,0:T(8,128)(2,1)} %bitcast.4, bf16[192,1024]{1,0:T(8,128)(2,1)} %bitcast.5), custom_call_target="tpu_custom_call" | custom-call | flops 704643072 | bytes 3670016 | tf_op jit(solution)/shard_map/routed_backward/pallas_call | solution.py:352
  45.9 2.6 %place_rows.1 = (bf16[128,4096]{1,0:T(8,128)(2,1)}, bf16[1,1024,384]{2,1,0:T(8,128)(2,1)}) custom-call(bf16[4,1,16,512]{3,2,1,0:T(8,128)(2,1)} %get-tuple-element.4.fin_hbm, s32[1,128]{1,0:T(1,128)} %bitcast.7, bf16[1,1024,384]{2,1,0:T(8,128)(2,1)} %get-tuple-element.5.gw_hbm), custom_call_target="tpu_custom_call" | custom-call | tf_op jit(solution)/shard_map/place_rows/pallas_call | solution.py:394

commit v5 on v4

--- a/solution.py
+++ b/solution.py
@@ -18,10 +18,12 @@
 
 def kernel(
     n_dp, windows,
-    tok_ref, dy_ref, slot_ref, gate_ref, gu_ref, down_ref,
-    fin_ref, gw_ref,
-    pick, buf, xall, part, prcv, dgrcv, dguall, dxs, across, sums, ret, back, fin, gut, downt,
-    s_pick, r_pick, s_ag, r_ag, s_rs, r_rs, s_dg, r_dg, s_cross, r_cross, s_ret, r_ret, s_fin, r_fin,
+    tok_hbm, dy_hbm, slot_hbm, gate_hbm, gu_hbm, down_hbm,
+    fin_ref, gw_hbm,
+    tok_ref, dy_ref, slot_ref, gate_ref, gu_ref, down_ref, gw_ref,
+    pick, buf, xall, part, prcv, dgrcv, dguall, dxs, across, sums, ret, gut, downt,
+    s_in, s_out,
+    s_pick, r_pick, s_ag, r_ag, s_rs, r_rs, s_dg, r_dg, s_cross, r_cross, s_ret, r_ret,
 ):
     S = GROUP
     Z = S // 2
@@ -42,22 +44,39 @@
     def member(z, y):
         return (me_d, me_w * S + z * 2 + y)
 
+    small = [
+        pltpu.make_async_copy(slot_hbm, slot_ref, s_in.at[0]),
+        pltpu.make_async_copy(gate_hbm, gate_ref, s_in.at[1]),
+    ]
+    big = []
+    for d in range(n_dp):
+        cut = pl.ds(d * cols, cols)
+        at = 4 + 2 * d
+        big.append(pltpu.make_async_copy(tok_hbm.at[:, cut], tok_ref.at[:, cut], s_in.at[at]))
+        big.append(pltpu.make_async_copy(dy_hbm.at[:, cut], dy_ref.at[:, cut], s_in.at[at + 1]))
+    down_in = pltpu.make_async_copy(down_hbm, down_ref, s_in.at[2])
+    gu_in = pltpu.make_async_copy(gu_hbm, gu_ref, s_in.at[3])
+    for copy in small + big + [down_in, gu_in]:
+        copy.start()
+
     barrier = pltpu.get_barrier_semaphore()
+    n_peer = n_same * Z
+    me_flat = (me_d * W + me_w) * Z + zz
+
+    def greet(k, carry):
+        flat = (me_flat + k) % n_peer
+        owner = flat // Z
+        target = (owner // W, (owner % W) * S + (flat % Z) * 2 + yy)
+        pl.semaphore_signal(barrier, inc=1, device_id=target, device_id_type=MESH)
+        return carry
+
+    lax.fori_loop(1, n_peer, greet, 0)
+    pl.semaphore_signal(barrier, inc=1, device_id=member(zz, 1 - yy), device_id_type=MESH)
 
     def same(k):
         flat = (me_d * W + me_w + k) % n_same
         return flat // W, flat % W
 
-    def other(k):
-        s = (me_s + k) % S
-        return s // 2, s % 2
-
-    for k in range(1, n_same):
-        d, w = same(k)
-        pl.semaphore_signal(barrier, inc=1, device_id=(d, w * S + me_s), device_id_type=MESH)
-    for k in range(1, S):
-        pl.semaphore_signal(barrier, inc=1, device_id=member(*other(k)), device_id_type=MESH)
-
     def pick_copy(h, d, w):
         return pltpu.make_async_remote_copy(
             src_ref=pick.at[h, d, w], dst_ref=buf.at[zz, yy, h, me_d, me_w],
@@ -72,6 +91,8 @@
             device_id=(d, w * S + me_s), device_id_type=MESH,
         )
 
+    for copy in small:
+        copy.wait()
     place = lax.broadcasted_iota(jnp.int32, (CAP, tokens), 0)
     sels, weights = [], []
     for e in range(W):
@@ -80,6 +101,8 @@
         weights.append(
             jnp.sum(jnp.where(hit, gate_ref[e : e + 1, :], 0.0), axis=1, keepdims=True)
         )
+    for copy in big:
+        copy.wait()
     for h in range(2):
         for e in range(W):
             for d in range(n_dp):
@@ -88,10 +111,11 @@
                 g = jnp.dot(sels[e], dy_ref[:, cut], preferred_element_type=F32) * weights[e]
                 pick[h, d, e] = jnp.concatenate([x, g], axis=0).astype(BF16)
         if h == 0:
-            pl.semaphore_wait(barrier, n_same - 1 + S - 1)
+            pl.semaphore_wait(barrier, n_peer)
         for k in range(1, n_same):
             pick_copy(h, *same(k)).start()
         buf[zz, yy, h, me_d, me_w] = pick[h, me_d, me_w]
+    down_in.wait()
     downt[...] = down_ref[...].T
 
     def spread(z, y, h, way, target):
@@ -122,12 +146,21 @@
             device_id=member(zz, 1 - yy), device_id_type=MESH,
         )
 
-    def return_copy(z, owner):
-        return pltpu.make_async_remote_copy(
-            src_ref=sums.at[z], dst_ref=ret.at[owner],
-            send_sem=s_ret.at[z], recv_sem=r_ret.at[owner],
-            device_id=member(z, yy), device_id_type=MESH,
-        )
+    def return_copy(z, d, w, owner_z, owner_d, owner_w):
+        return pltpu.make_async_remote_copy(
+            src_ref=sums.at[z, d, w], dst_ref=ret.at[owner_z, owner_d, owner_w],
+            send_sem=s_ret.at[z, d, w], recv_sem=r_ret.at[owner_z, owner_d, owner_w],
+            device_id=(d, w * S + z * 2 + yy), device_id_type=MESH,
+        )
+
+    def returns(z, act):
+        for k in range(1, n_same):
+            d, w = same(k)
+            act(return_copy(z, d, w, zz, me_d, me_w))
+
+        @pl.when(z != zz)
+        def _():
+            act(return_copy(z, me_d, me_w, zz, me_d, me_w))
 
     near = jnp.minimum(zz, Z - 1 - zz)
 
@@ -217,11 +250,10 @@
     def combine(m):
         z = nth(m)
         cross_copy(z).wait_recv()
-        sums[z] = (dxs[z, yy].astype(F32) + across[z].astype(F32)).astype(BF16)
-
-        @pl.when(m > 0)
-        def _():
-            return_copy(z, zz).start()
+        both = dxs[z, yy].astype(F32) + across[z].astype(F32)
+        both = both.reshape(n_dp, W, CAP, cols)
+        sums[z] = jnp.concatenate([both[..., :half], both[..., half:]], axis=2).astype(BF16)
+        returns(z, start)
 
     def step(m, carry):
         @pl.when(m < Z)
@@ -248,6 +280,7 @@
         for k in range(1, n_same):
             pick_arrival(h, *same(k)).wait_recv()
         forward(zz, h, start)
+    gu_in.wait()
     gut[...] = gu_ref[...].T
     pass_on(1, 0)
     lax.fori_loop(0, Z + 2, step, 0)
@@ -259,37 +292,19 @@
             preferred_element_type=F32,
         ).astype(BF16)
 
+    def gradient_out(h):
+        cut = pl.ds(h * half, half)
+        return pltpu.make_async_copy(gw_ref.at[0, cut], gw_hbm.at[0, cut], s_out.at[h])
+
     weight_gradient(0)
+    gradient_out(0).start()
     combine(Z - 1)
     weight_gradient(1)
-
-    total = sums[zz].astype(F32)
-    for k in range(1, Z):
-        z = (zz + k) % Z
-        return_copy(z, z).wait_recv()
-        total = total + ret[z].astype(F32)
-    total = total.reshape(n_dp, W, CAP, cols)
-    back[...] = jnp.concatenate(
-        [total[..., : cols // 2], total[..., cols // 2 :]], axis=2
-    ).astype(BF16)
-
-    def fin_copy(d, w, owner_d, owner_w):
-        return pltpu.make_async_remote_copy(
-            src_ref=back.at[d, w], dst_ref=fin.at[owner_d, owner_w],
-            send_sem=s_fin.at[d, w], recv_sem=r_fin.at[owner_d, owner_w],
-            device_id=(d, w * S + me_s), device_id_type=MESH,
-        )
-
-    for k in range(1, n_same):
-        d, w = same(k)
-        fin_copy(d, w, me_d, me_w).start()
-    fin[me_d, me_w] = back[me_d, me_w]
+    gradient_out(1).start()
 
     for k in range(1, n_same):
         for h in range(2):
             pick_copy(h, *same(k)).wait_send()
-    for k in range(1, Z):
-        return_copy((zz + k) % Z, zz).wait_send()
 
     def wait_send(copy):
         copy.wait_send()
@@ -302,41 +317,60 @@
             d = (me_d + k) % n_dp
             reduce_copy(z, d, me_d).wait_send()
             share_copy(z, d, me_d).wait_send()
+        returns(z, wait_send)
         return carry
 
     lax.fori_loop(0, Z, drain, 0)
-    for k in range(1, n_same):
-        d, w = same(k)
-        fin_copy(d, w, d, w).wait_recv()
-        fin_copy(d, w, me_d, me_w).wait_send()
-    fin_ref[...] = fin[...]
-
-
-def place_rows(fin_hbm, slot_hbm, gw_hbm, gx_ref, gw_ref, fin_ref, slot_ref, sems):
+
+    total = 0.0
+    ret[zz, me_d, me_w] = sums[zz, me_d, me_w]
+    for j in range(Z):
+        z = (zz + j) % Z
+        for k in range(1 if j == 0 else 0, n_same):
+            d, w = same(k)
+            return_copy(z, d, w, z, d, w).wait_recv()
+        total = total + ret[z].astype(F32)
+    fin_ref[...] = total.astype(BF16)
+    gradient_out(0).wait()
+    gradient_out(1).wait()
+
+
+def place_rows(
+    fin_hbm, slot_hbm, gw_in, gx_hbm, gw_hbm, fin_ref, slot_ref, gx_ref, gw_ref, s_in, s_out
+):
     n_dp, W, _, half = fin_ref.shape
     tokens = gx_ref.shape[0]
-    copies = [
-        pltpu.make_async_copy(slot_hbm, slot_ref, sems.at[0]),
-        pltpu.make_async_copy(fin_hbm, fin_ref, sems.at[1]),
-        pltpu.make_async_copy(gw_hbm, gw_ref, sems.at[2]),
-    ]
-    for copy in copies:
+    slot_copy = pltpu.make_async_copy(slot_hbm, slot_ref, s_in.at[0])
+    fin_copy = pltpu.make_async_copy(fin_hbm, fin_ref, s_in.at[1])
+    gw_copy = pltpu.make_async_copy(gw_in, gw_ref, s_in.at[2])
+    for copy in (slot_copy, fin_copy, gw_copy):
         copy.start()
-    copies[0].wait()
-    copies[1].wait()
+    gw_out = pltpu.make_async_copy(gw_ref, gw_hbm, s_in.at[3])
+    outs = []
+    slot_copy.wait()
     place = lax.broadcasted_iota(jnp.int32, (2 * CAP, tokens), 0)
+    hits = []
     for h in range(2):
-        hits = []
         for e in range(W):
             hit = (slot_ref[e : e + 1, :] == place - h * CAP) & (place >= h * CAP)
             hits.append(jnp.where(hit, 1.0, 0.0).T.astype(BF16))
-        for d in range(n_dp):
-            out = jnp.dot(hits[0], fin_ref[d, 0], preferred_element_type=F32)
+    fin_copy.wait()
+    for d in range(n_dp):
+        for h in range(2):
+            out = jnp.dot(hits[h * W], fin_ref[d, 0], preferred_element_type=F32)
             for e in range(1, W):
-                out = out + jnp.dot(hits[e], fin_ref[d, e], preferred_element_type=F32)
+                out = out + jnp.dot(hits[h * W + e], fin_ref[d, e], preferred_element_type=F32)
             at = (2 * d + h) * half
             gx_ref[:, at : at + half] = out.astype(BF16)
-    copies[2].wait()
+        cut = pl.ds(2 * d * half, 2 * half)
+        outs.append(pltpu.make_async_copy(gx_ref.at[:, cut], gx_hbm.at[:, cut], s_out.at[d]))
+        outs[d].start()
+        if d == 0:
+            gw_copy.wait()
+            gw_out.start()
+    for copy in outs:
+        copy.wait()
+    gw_out.wait()
 
 
 def on_device(n_dp, tokens, output_gradient, slot, gate_weight, gate_up_weight, down_weight):
@@ -347,6 +381,7 @@
     hidden = wide // 2
     rows = n_dp * W * CAP
     vmem = pl.BlockSpec(memory_space=pltpu.VMEM)
+    anywhere = pl.BlockSpec(memory_space=pl.ANY)
     dma = pltpu.SemaphoreType.DMA
     slot_row = slot.T
     fin, grad_gate_up = pl.pallas_call(
@@ -355,9 +390,16 @@
             jax.ShapeDtypeStruct((n_dp, W, 2 * CAP, cols // 2), BF16),
             jax.ShapeDtypeStruct(gate_up_weight.shape, BF16),
         ),
-        in_specs=[vmem] * 6,
-        out_specs=(vmem, vmem),
+        in_specs=[anywhere] * 6,
+        out_specs=(vmem, anywhere),
         scratch_shapes=[
+            pltpu.VMEM(tokens.shape, BF16),
+            pltpu.VMEM(tokens.shape, BF16),
+            pltpu.VMEM(slot_row.shape, jnp.int32),
+            pltpu.VMEM(slot_row.shape, F32),
+            pltpu.VMEM((cols, wide), BF16),
+            pltpu.VMEM((hidden, cols), BF16),
+            pltpu.VMEM((1, cols, wide), BF16),
             pltpu.VMEM((2, n_dp, W, 2 * CAP, cols // 2), BF16),
             pltpu.VMEM((Z, 2, 2, n_dp, W, 2 * CAP, cols // 2), BF16),
             pltpu.VMEM((Z, 2 * rows, cols), BF16),
@@ -367,19 +409,17 @@
             pltpu.VMEM((Z, 2 * rows, wide), BF16),
             pltpu.VMEM((Z, 2, rows, cols), BF16),
             pltpu.VMEM((Z, rows, cols), BF16),
-            pltpu.VMEM((Z, rows, cols), BF16),
-            pltpu.VMEM((Z, rows, cols), BF16),
-            pltpu.VMEM((n_dp, W, 2 * CAP, cols // 2), BF16),
-            pltpu.VMEM((n_dp, W, 2 * CAP, cols // 2), BF16),
+            pltpu.VMEM((Z, n_dp, W, 2 * CAP, cols // 2), BF16),
+            pltpu.VMEM((Z, n_dp, W, 2 * CAP, cols // 2), BF16),
             pltpu.VMEM((wide, cols), BF16),
             pltpu.VMEM((cols, hidden), BF16),
+            dma((4 + 2 * n_dp,)), dma((2,)),
             dma((2, n_dp, W)), dma((2, n_dp, W)),
             dma((Z, 2, 3)), dma((Z, 2, 2)),
             dma((Z, n_dp)), dma((Z, n_dp)),
             dma((Z, n_dp)), dma((Z, n_dp)),
             dma((Z,)), dma((Z,)),
-            dma((Z,)), dma((Z,)),
-            dma((n_dp, W)), dma((n_dp, W)),
+            dma((Z, n_dp, W)), dma((Z, n_dp, W)),
         ],
         compiler_params=pltpu.CompilerParams(
             collective_id=0, has_side_effects=True, vmem_limit_bytes=58 * 1024 * 1024
@@ -390,7 +430,6 @@
         ),
         name="routed_backward",
     )(tokens, output_gradient, slot_row, gate_weight.T, gate_up_weight[0], down_weight[0])
-    anywhere = pl.BlockSpec(memory_space=pl.ANY)
     return pl.pallas_call(
         place_rows,
         out_shape=(
@@ -398,11 +437,13 @@
             jax.ShapeDtypeStruct(gate_up_weight.shape, BF16),
         ),
         in_specs=[anywhere] * 3,
-        out_specs=(vmem, vmem),
+        out_specs=(anywhere, anywhere),
         scratch_shapes=[
             pltpu.VMEM(fin.shape, BF16),
             pltpu.VMEM(slot_row.shape, jnp.int32),
-            dma((3,)),
+            pltpu.VMEM(tokens.shape, BF16),
+            pltpu.VMEM(gate_up_weight.shape, BF16),
+            dma((4,)), dma((n_dp,)),
         ],
         compiler_params=pltpu.CompilerParams(vmem_limit_bytes=58 * 1024 * 1024),
         name="place_rows",

time: 48.7 us -> 44 us (0.903)
  Pallas kernels: 47.9 us -> 43.2 us
    pallas_call x1, Pallas kernels: 45.3 us -> 40.8 us  [on_device(): pl.pallas_call(functools.partial(kernel, n_dp, W), out_shape=(jax.ShapeDt...]
where the time goes in v5:
time: 44 us; the launch traced here: 43.8 us
  Pallas kernels  43.2 us (98%)
  between operations  0.64 us (1%)
    pallas_call x1, Pallas kernels, on_device(): pl.pallas_call(functools.partial(kernel, n_dp, W), out_shape=(jax.ShapeDt...  40.8 us
    pallas_call x1, Pallas kernels, on_device(): pl.pallas_call(place_rows, out_shape=(jax.ShapeDtypeStruct(tokens.shape,...  2.39 us

profile of v5, /device:TPU:0, one launch (start us, length us, event | category | flops | bytes accessed | tf_op | source)
XLA Modules:
  0.0 43.8 jit_solution(13961476099626894820)
XLA Ops:
  0.6 40.8 %routed_backward.1 = (bf16[4,1,16,512]{3,2,1,0:T(8,128)(2,1)}, bf16[1,1024,384]{2,1,0:T(8,128)(2,1)}) custom-call(bf16[128,4096]{1,0:T(8,128)(2,1)} %tok_hbm.1, bf16[128,4096]{1,0:T(8,128)(2,1)} %dy_hbm.1, s32[1,128]{1,0:T(1,128)} %bitcast.6, f32[1,128]{1,0:T(1,128)} %bitcast.8, bf16[1024,384]{1,0:T(8,128)(2,1)} %bitcast.4, bf16[192,1024]{1,0:T(8,128)(2,1)} %bitcast.5), custom_call_target="tpu_custom_call" | custom-call | flops 704643072 | bytes 3670016 | tf_op jit(solution)/shard_map/routed_backward/pallas_call | solution.py:387
  41.4 2.4 %place_rows.1 = (bf16[128,4096]{1,0:T(8,128)(2,1)}, bf16[1,1024,384]{2,1,0:T(8,128)(2,1)}) custom-call(bf16[4,1,16,512]{3,2,1,0:T(8,128)(2,1)} %get-tuple-element.4.fin_hbm, s32[1,128]{1,0:T(1,128)} %bitcast.7, bf16[1,1024,384]{2,1,0:T(8,128)(2,1)} %get-tuple-element.5.gw_in), custom_call_target="tpu_custom_call" | custom-call | tf_op jit(solution)/shard_map/place_rows/pallas_call | solution.py:433

commit v6 on v5

--- a/solution.py
+++ b/solution.py
@@ -179,7 +179,22 @@
         def _():
             act(spread(z, yy, h, 1, (zz - 1, yy)))
 
-        act(spread(z, yy, h, 2, (zz, 1 - yy)))
+        if h == 0:
+            act(spread(z, yy, h, 2, (zz, 1 - yy)))
+        else:
+
+            @pl.when((z - zz != 1) & (zz - z != 1))
+            def _():
+                act(spread(z, yy, h, 2, (zz, 1 - yy)))
+
+    def forward_other(act):
+        @pl.when(zz + 1 < Z)
+        def _():
+            act(spread(zz, 1 - yy, 1, 3, (zz + 1, yy)))
+
+        @pl.when(zz >= 1)
+        def _():
+            act(spread(zz, 1 - yy, 1, 4, (zz - 1, yy)))
 
     def start(copy):
         copy.start()
@@ -200,6 +215,12 @@
         a_u = dh = 0.0
         for h in range(2):
             spread(z, 1 - yy, h, 2, (zz, 1 - yy)).wait_recv()
+            if h == 1:
+
+                @pl.when(m == 0)
+                def _():
+                    forward_other(start)
+
             both = buf[z, :, h].astype(F32).reshape(2 * n_dp * W, 2, CAP, half)
             x = both[:, 0].reshape(2 * rows, half).astype(BF16)
             g = both[:, 1].reshape(2 * rows, half).astype(BF16)
@@ -320,6 +341,7 @@
         returns(z, wait_send)
         return carry
 
+    forward_other(wait_send)
     lax.fori_loop(0, Z, drain, 0)
 
     total = 0.0
@@ -336,16 +358,15 @@
 
 
 def place_rows(
-    fin_hbm, slot_hbm, gw_in, gx_hbm, gw_hbm, fin_ref, slot_ref, gx_ref, gw_ref, s_in, s_out
+    fin_hbm, slot_hbm, gw_in, gx_hbm, gw_hbm, fin_ref, slot_ref, gx_ref, s_in, s_out
 ):
     n_dp, W, _, half = fin_ref.shape
     tokens = gx_ref.shape[0]
     slot_copy = pltpu.make_async_copy(slot_hbm, slot_ref, s_in.at[0])
     fin_copy = pltpu.make_async_copy(fin_hbm, fin_ref, s_in.at[1])
-    gw_copy = pltpu.make_async_copy(gw_in, gw_ref, s_in.at[2])
+    gw_copy = pltpu.make_async_copy(gw_in, gw_hbm, s_in.at[2])
     for copy in (slot_copy, fin_copy, gw_copy):
         copy.start()
-    gw_out = pltpu.make_async_copy(gw_ref, gw_hbm, s_in.at[3])
     outs = []
     slot_copy.wait()
     place = lax.broadcasted_iota(jnp.int32, (2 * CAP, tokens), 0)
@@ -365,12 +386,9 @@
         cut = pl.ds(2 * d * half, 2 * half)
         outs.append(pltpu.make_async_copy(gx_ref.at[:, cut], gx_hbm.at[:, cut], s_out.at[d]))
         outs[d].start()
-        if d == 0:
-            gw_copy.wait()
-            gw_out.start()
     for copy in outs:
         copy.wait()
-    gw_out.wait()
+    gw_copy.wait()
 
 
 def on_device(n_dp, tokens, output_gradient, slot, gate_weight, gate_up_weight, down_weight):
@@ -415,7 +433,7 @@
             pltpu.VMEM((cols, hidden), BF16),
             dma((4 + 2 * n_dp,)), dma((2,)),
             dma((2, n_dp, W)), dma((2, n_dp, W)),
-            dma((Z, 2, 3)), dma((Z, 2, 2)),
+            dma((Z, 2, 5)), dma((Z, 2, 2)),
             dma((Z, n_dp)), dma((Z, n_dp)),
             dma((Z, n_dp)), dma((Z, n_dp)),
             dma((Z,)), dma((Z,)),
@@ -442,8 +460,7 @@
             pltpu.VMEM(fin.shape, BF16),
             pltpu.VMEM(slot_row.shape, jnp.int32),
             pltpu.VMEM(tokens.shape, BF16),
-            pltpu.VMEM(gate_up_weight.shape, BF16),
-            dma((4,)), dma((n_dp,)),
+            dma((3,)), dma((n_dp,)),
         ],
         compiler_params=pltpu.CompilerParams(vmem_limit_bytes=58 * 1024 * 1024),
         name="place_rows",

time: 44 us -> 66.9 us (1.52)
  Pallas kernels: 43.2 us -> 66.1 us
    pallas_call x1, Pallas kernels: 2.39 us -> 25 us  [on_device(): pl.pallas_call(place_rows, out_shape=(jax.ShapeDtypeStruct(tokens.shape,...]
where the time goes in v6:
time: 66.9 us; the launch traced here: 66.7 us
  Pallas kernels  66.1 us (99%)
    pallas_call x1, Pallas kernels, on_device(): pl.pallas_call(functools.partial(kernel, n_dp, W), out_shape=(jax.ShapeDt...  41.1 us
    pallas_call x1, Pallas kernels, on_device(): pl.pallas_call(place_rows, out_shape=(jax.ShapeDtypeStruct(tokens.shape,...  25 us

profile of v6, /device:TPU:0, one launch (start us, length us, event | category | flops | bytes accessed | tf_op | source)
XLA Modules:
  0.0 66.7 jit_solution(108573675750350149)
XLA Ops:
  0.6 41.1 %routed_backward.1 = (bf16[4,1,16,512]{3,2,1,0:T(8,128)(2,1)}, bf16[1,1024,384]{2,1,0:T(8,128)(2,1)}) custom-call(bf16[128,4096]{1,0:T(8,128)(2,1)} %tok_hbm.1, bf16[128,4096]{1,0:T(8,128)(2,1)} %dy_hbm.1, s32[1,128]{1,0:T(1,128)} %bitcast.6, f32[1,128]{1,0:T(1,128)} %bitcast.8, bf16[1024,384]{1,0:T(8,128)(2,1)} %bitcast.4, bf16[192,1024]{1,0:T(8,128)(2,1)} %bitcast.5), custom_call_target="tpu_custom_call" | custom-call | flops 704643072 | bytes 3670016 | tf_op jit(solution)/shard_map/routed_backward/pallas_call | solution.py:405
  41.7 25.0 %place_rows.1 = (bf16[128,4096]{1,0:T(8,128)(2,1)}, bf16[1,1024,384]{2,1,0:T(8,128)(2,1)}) custom-call(bf16[4,1,16,512]{3,2,1,0:T(8,128)(2,1)} %get-tuple-element.4.fin_hbm, s32[1,128]{1,0:T(1,128)} %bitcast.7, bf16[1,1024,384]{2,1,0:T(8,128)(2,1)} %get-tuple-element.5.gw_in), custom_call_target="tpu_custom_call" | custom-call | tf_op jit(solution)/shard_map/place_rows/pallas_call | solution.py:451

commit v7 on v6

--- a/solution.py
+++ b/solution.py
@@ -171,11 +171,11 @@
         return zz + jnp.where(m <= 2 * near, alternating, beyond)
 
     def forward(z, h, act):
-        @pl.when((z <= zz) & (zz + 1 < Z))
+        @pl.when((z <= zz) & (zz + 1 < Z) & (zz - z < Z - 2))
         def _():
             act(spread(z, yy, h, 0, (zz + 1, yy)))
 
-        @pl.when((z >= zz) & (zz >= 1))
+        @pl.when((z >= zz) & (zz >= 1) & (z - zz < Z - 2))
         def _():
             act(spread(z, yy, h, 1, (zz - 1, yy)))
 
@@ -195,6 +195,15 @@
         @pl.when(zz >= 1)
         def _():
             act(spread(zz, 1 - yy, 1, 4, (zz - 1, yy)))
+
+    def forward_far(h, act):
+        @pl.when(zz == 0)
+        def _():
+            act(spread(zz, yy, h, 5, (Z - 1, yy)))
+
+        @pl.when(zz == Z - 1)
+        def _():
+            act(spread(zz, yy, h, 5, (0, yy)))
 
     def start(copy):
         copy.start()
@@ -301,6 +310,8 @@
         for k in range(1, n_same):
             pick_arrival(h, *same(k)).wait_recv()
         forward(zz, h, start)
+    for h in range(2):
+        forward_far(h, start)
     gu_in.wait()
     gut[...] = gu_ref[...].T
     pass_on(1, 0)
@@ -342,6 +353,8 @@
         return carry
 
     forward_other(wait_send)
+    for h in range(2):
+        forward_far(h, wait_send)
     lax.fori_loop(0, Z, drain, 0)
 
     total = 0.0
@@ -358,15 +371,16 @@
 
 
 def place_rows(
-    fin_hbm, slot_hbm, gw_in, gx_hbm, gw_hbm, fin_ref, slot_ref, gx_ref, s_in, s_out
+    fin_hbm, slot_hbm, gw_in, gx_hbm, gw_hbm, fin_ref, slot_ref, gx_ref, gw_ref, s_in, s_out
 ):
     n_dp, W, _, half = fin_ref.shape
     tokens = gx_ref.shape[0]
     slot_copy = pltpu.make_async_copy(slot_hbm, slot_ref, s_in.at[0])
     fin_copy = pltpu.make_async_copy(fin_hbm, fin_ref, s_in.at[1])
-    gw_copy = pltpu.make_async_copy(gw_in, gw_hbm, s_in.at[2])
+    gw_copy = pltpu.make_async_copy(gw_in, gw_ref, s_in.at[2])
     for copy in (slot_copy, fin_copy, gw_copy):
         copy.start()
+    gw_out = pltpu.make_async_copy(gw_ref, gw_hbm, s_in.at[3])
     outs = []
     slot_copy.wait()
     place = lax.broadcasted_iota(jnp.int32, (2 * CAP, tokens), 0)
@@ -375,6 +389,8 @@
         for e in range(W):
             hit = (slot_ref[e : e + 1, :] == place - h * CAP) & (place >= h * CAP)
             hits.append(jnp.where(hit, 1.0, 0.0).T.astype(BF16))
+    gw_copy.wait()
+    gw_out.start()
     fin_copy.wait()
     for d in range(n_dp):
         for h in range(2):
@@ -388,7 +404,7 @@
         outs[d].start()
     for copy in outs:
         copy.wait()
-    gw_copy.wait()
+    gw_out.wait()
 
 
 def on_device(n_dp, tokens, output_gradient, slot, gate_weight, gate_up_weight, down_weight):
@@ -433,7 +449,7 @@
             pltpu.VMEM((cols, hidden), BF16),
             dma((4 + 2 * n_dp,)), dma((2,)),
             dma((2, n_dp, W)), dma((2, n_dp, W)),
-            dma((Z, 2, 5)), dma((Z, 2, 2)),
+            dma((Z, 2, 6)), dma((Z, 2, 2)),
             dma((Z, n_dp)), dma((Z, n_dp)),
             dma((Z, n_dp)), dma((Z, n_dp)),
             dma((Z,)), dma((Z,)),
@@ -460,7 +476,8 @@
             pltpu.VMEM(fin.shape, BF16),
             pltpu.VMEM(slot_row.shape, jnp.int32),
             pltpu.VMEM(tokens.shape, BF16),
-            dma((3,)), dma((n_dp,)),
+            pltpu.VMEM(gate_up_weight.shape, BF16),
+            dma((4,)), dma((n_dp,)),
         ],
         compiler_params=pltpu.CompilerParams(vmem_limit_bytes=58 * 1024 * 1024),
         name="place_rows",

time: 66.9 us -> 46.3 us (0.69)
  Pallas kernels: 66.1 us -> 45.5 us
    pallas_call x1, Pallas kernels: 25 us -> 2.48 us  [on_device(): pl.pallas_call(place_rows, out_shape=(jax.ShapeDtypeStruct(tokens.shape,...]
    pallas_call x1, Pallas kernels: 41.1 us -> 43 us  [on_device(): pl.pallas_call(functools.partial(kernel, n_dp, W), out_shape=(jax.ShapeDt...]
where the time goes in v7:
time: 46.3 us; the launch traced here: 46.2 us
  Pallas kernels  45.5 us (98%)
  between operations  0.64 us (1%)
    pallas_call x1, Pallas kernels, on_device(): pl.pallas_call(functools.partial(kernel, n_dp, W), out_shape=(jax.ShapeDt...  43 us
    pallas_call x1, Pallas kernels, on_device(): pl.pallas_call(place_rows, out_shape=(jax.ShapeDtypeStruct(tokens.shape,...  2.48 us

profile of v7, /device:TPU:0, one launch (start us, length us, event | category | flops | bytes accessed | tf_op | source)
XLA Modules:
  0.0 46.2 jit_solution(17314257912214371789)
XLA Ops:
  0.6 43.0 %routed_backward.1 = (bf16[4,1,16,512]{3,2,1,0:T(8,128)(2,1)}, bf16[1,1024,384]{2,1,0:T(8,128)(2,1)}) custom-call(bf16[128,4096]{1,0:T(8,128)(2,1)} %tok_hbm.1, bf16[128,4096]{1,0:T(8,128)(2,1)} %dy_hbm.1, s32[1,128]{1,0:T(1,128)} %bitcast.6, f32[1,128]{1,0:T(1,128)} %bitcast.8, bf16[1024,384]{1,0:T(8,128)(2,1)} %bitcast.4, bf16[192,1024]{1,0:T(8,128)(2,1)} %bitcast.5), custom_call_target="tpu_custom_call" | custom-call | flops 704643072 | bytes 3670016 | tf_op jit(solution)/shard_map/routed_backward/pallas_call | solution.py:421
  43.7 2.5 %place_rows.1 = (bf16[128,4096]{1,0:T(8,128)(2,1)}, bf16[1,1024,384]{2,1,0:T(8,128)(2,1)}) custom-call(bf16[4,1,16,512]{3,2,1,0:T(8,128)(2,1)} %get-tuple-element.4.fin_hbm, s32[1,128]{1,0:T(1,128)} %bitcast.7, bf16[1,1024,384]{2,1,0:T(8,128)(2,1)} %get-tuple-element.5.gw_in), custom_call_target="tpu_custom_call" | custom-call | tf_op jit(solution)/shard_map/place_rows/pallas_call | solution.py:467

commit v8 on v6

--- a/solution.py
+++ b/solution.py
@@ -101,19 +101,24 @@
         weights.append(
             jnp.sum(jnp.where(hit, gate_ref[e : e + 1, :], 0.0), axis=1, keepdims=True)
         )
-    for copy in big:
-        copy.wait()
-    for h in range(2):
-        for e in range(W):
-            for d in range(n_dp):
-                cut = slice(d * cols + h * half, d * cols + (h + 1) * half)
+    for d in range(n_dp):
+        big[2 * d].wait()
+        big[2 * d + 1].wait()
+        for h in range(2):
+            cut = slice(d * cols + h * half, d * cols + (h + 1) * half)
+            for e in range(W):
                 x = jnp.dot(sels[e], tok_ref[:, cut], preferred_element_type=F32)
                 g = jnp.dot(sels[e], dy_ref[:, cut], preferred_element_type=F32) * weights[e]
                 pick[h, d, e] = jnp.concatenate([x, g], axis=0).astype(BF16)
-        if h == 0:
-            pl.semaphore_wait(barrier, n_peer)
-        for k in range(1, n_same):
-            pick_copy(h, *same(k)).start()
+            if d == 0 and h == 0:
+                pl.semaphore_wait(barrier, n_peer)
+            for e in range(W):
+
+                @pl.when((me_d != d) | (me_w != e))
+                def _():
+                    pick_copy(h, d, e).start()
+
+    for h in range(2):
         buf[zz, yy, h, me_d, me_w] = pick[h, me_d, me_w]
     down_in.wait()
     downt[...] = down_ref[...].T
@@ -358,15 +363,16 @@
 
 
 def place_rows(
-    fin_hbm, slot_hbm, gw_in, gx_hbm, gw_hbm, fin_ref, slot_ref, gx_ref, s_in, s_out
+    fin_hbm, slot_hbm, gw_in, gx_hbm, gw_hbm, fin_ref, slot_ref, gx_ref, gw_ref, s_in, s_out
 ):
     n_dp, W, _, half = fin_ref.shape
     tokens = gx_ref.shape[0]
     slot_copy = pltpu.make_async_copy(slot_hbm, slot_ref, s_in.at[0])
     fin_copy = pltpu.make_async_copy(fin_hbm, fin_ref, s_in.at[1])
-    gw_copy = pltpu.make_async_copy(gw_in, gw_hbm, s_in.at[2])
+    gw_copy = pltpu.make_async_copy(gw_in, gw_ref, s_in.at[2])
     for copy in (slot_copy, fin_copy, gw_copy):
         copy.start()
+    gw_out = pltpu.make_async_copy(gw_ref, gw_hbm, s_in.at[3])
     outs = []
     slot_copy.wait()
     place = lax.broadcasted_iota(jnp.int32, (2 * CAP, tokens), 0)
@@ -375,6 +381,8 @@
         for e in range(W):
             hit = (slot_ref[e : e + 1, :] == place - h * CAP) & (place >= h * CAP)
             hits.append(jnp.where(hit, 1.0, 0.0).T.astype(BF16))
+    gw_copy.wait()
+    gw_out.start()
     fin_copy.wait()
     for d in range(n_dp):
         for h in range(2):
@@ -388,7 +396,7 @@
         outs[d].start()
     for copy in outs:
         copy.wait()
-    gw_copy.wait()
+    gw_out.wait()
 
 
 def on_device(n_dp, tokens, output_gradient, slot, gate_weight, gate_up_weight, down_weight):
@@ -460,7 +468,8 @@
             pltpu.VMEM(fin.shape, BF16),
             pltpu.VMEM(slot_row.shape, jnp.int32),
             pltpu.VMEM(tokens.shape, BF16),
-            dma((3,)), dma((n_dp,)),
+            pltpu.VMEM(gate_up_weight.shape, BF16),
+            dma((4,)), dma((n_dp,)),
         ],
         compiler_params=pltpu.CompilerParams(vmem_limit_bytes=58 * 1024 * 1024),
         name="place_rows",

time: 66.9 us -> 45.7 us (0.68)
  Pallas kernels: 66.1 us -> 44.9 us
    pallas_call x1, Pallas kernels: 25 us -> 2.48 us  [on_device(): pl.pallas_call(place_rows, out_shape=(jax.ShapeDtypeStruct(tokens.shape,...]
    pallas_call x1, Pallas kernels: 41.1 us -> 42.4 us  [on_device(): pl.pallas_call(functools.partial(kernel, n_dp, W), out_shape=(jax.ShapeDt...]
where the time goes in v8:
time: 45.7 us; the launch traced here: 45.5 us
  Pallas kernels  44.9 us (98%)
  between operations  0.64 us (1%)
    pallas_call x1, Pallas kernels, on_device(): pl.pallas_call(functools.partial(kernel, n_dp, W), out_shape=(jax.ShapeDt...  42.4 us
    pallas_call x1, Pallas kernels, on_device(): pl.pallas_call(place_rows, out_shape=(jax.ShapeDtypeStruct(tokens.shape,...  2.48 us

profile of v8, /device:TPU:0, one launch (start us, length us, event | category | flops | bytes accessed | tf_op | source)
XLA Modules:
  0.0 45.5 jit_solution(1135478756257105404)
XLA Ops:
  0.6 42.4 %routed_backward.1 = (bf16[4,1,16,512]{3,2,1,0:T(8,128)(2,1)}, bf16[1,1024,384]{2,1,0:T(8,128)(2,1)}) custom-call(bf16[128,4096]{1,0:T(8,128)(2,1)} %tok_hbm.1, bf16[128,4096]{1,0:T(8,128)(2,1)} %dy_hbm.1, s32[1,128]{1,0:T(1,128)} %bitcast.6, f32[1,128]{1,0:T(1,128)} %bitcast.8, bf16[1024,384]{1,0:T(8,128)(2,1)} %bitcast.4, bf16[192,1024]{1,0:T(8,128)(2,1)} %bitcast.5), custom_call_target="tpu_custom_call" | custom-call | flops 704643072 | bytes 3670016 | tf_op jit(solution)/shard_map/routed_backward/pallas_call | solution.py:413
  43.0 2.5 %place_rows.1 = (bf16[128,4096]{1,0:T(8,128)(2,1)}, bf16[1,1024,384]{2,1,0:T(8,128)(2,1)}) custom-call(bf16[4,1,16,512]{3,2,1,0:T(8,128)(2,1)} %get-tuple-element.4.fin_hbm, s32[1,128]{1,0:T(1,128)} %bitcast.7, bf16[1,1024,384]{2,1,0:T(8,128)(2,1)} %get-tuple-element.5.gw_in), custom_call_target="tpu_custom_call" | custom-call | tf_op jit(solution)/shard_map/place_rows/pallas_call | solution.py:459
